TPU v7x, 256 devices: a whole 4x4x8 slice. The times are simulated.
256 devices in a mesh: tm: 4 (over x_lo, core), space: 64 (over z, y, x_hi).
Axes of the slice: x: 4 (x_hi: 2, x_lo: 2; x = x_hi * 2 + x_lo), y: 4, z: 8, core: 2. Of those that a mesh axis runs over, the one named last changes fastest.
Arguments:
- adjoint_end: float32 [8, 16384, 1024], P('tm', 'space'), may hold values from -6 to 6
- adjoint_source: float32 [8, 2, 16384, 1024], P('tm', None, 'space'), may hold values from -6 to 6
- region: int32 [16384, 1024], P('space'), may hold values from 0 to 7
- dirichlet: int32 [16384, 1024], P('space'), may hold values 0 or 1
- reluctivity: float32 [8], replicated, may hold values from 0.5 to 8
- conductance: float32 [8], replicated, may hold values from 0 to 2
Outputs:
- new_end: float32 [8, 16384, 1024], P('tm', 'space')
All inputs are finite; a program needn't handle non-finite values. No bound on the sum of `dirichlet` on one device may be relied on, other than what follows from the above.
Results may differ from a plain program's by a relative error of at most 0.00002.
Values sent between devices are 32-bit elements; how exact they have to be, the bound alone decides.
No kernel may reach another device: no remote copies, remote signals or barrier semaphores. Data moves between devices by JAX's collectives and lax.ppermute only.
A program may use at most 128 MiB of HBM per device.

v0:
```python
import math

import jax
import jax.numpy as jnp
from jax import lax
from jax.sharding import PartitionSpec as P

SWEEPS = 2


relaxation = 0.8


def extended(shard, sides, width):
    for axis, dim in sides:
        devices, length = (lax.axis_size(axis), shard.shape[dim])
        up = [(i, (i + 1) % devices) for i in range(devices)]
        down = [(j, i) for i, j in up]
        last = lax.slice_in_dim(shard, length - width, length, axis=dim)
        leading = lax.slice_in_dim(shard, 0, width, axis=dim)
        before = lax.ppermute(last, axis, up)
        after = lax.ppermute(leading, axis, down)
        shard = jnp.concatenate([before, shard, after], axis=dim)
    return shard


def from_behind(shard, axis, by):
    devices = lax.axis_size(axis)
    return lax.ppermute(shard, axis, [(i, (i + by) % devices) for i in range(devices)])


def lookup(region, table):
    result = jnp.zeros(region.shape, table.dtype)
    for entry in range(table.shape[0]):
        result = jnp.where(region == entry, table[entry], result)
    return result


def face_weights(reluct_pad, mass_term, spacing):
    radial = reluct_pad.shape[-1]
    position = jnp.arange(radial, dtype=jnp.float32)
    cycle_factor = 1.0 + position * spacing
    outer_factor = 1.0 + (position + 0.5) * spacing
    inner_factor = 1.0 + (position - 0.5) * spacing
    centre = reluct_pad[1:-1]
    west_face = 0.5 * (centre + reluct_pad[:-2]) / cycle_factor
    east_face = 0.5 * (centre + reluct_pad[2:]) / cycle_factor
    upward = jnp.concatenate([centre[:, 1:], centre[:, -1:]], axis=1)
    downward = jnp.concatenate([centre[:, :1], centre[:, :-1]], axis=1)
    outer_face = 0.5 * (centre + upward) * outer_factor
    inner_face = 0.5 * (centre + downward) * inner_factor
    diagonal = mass_term + west_face + east_face + outer_face + inner_face
    return (west_face, east_face, outer_face, inner_face, diagonal, relaxation / diagonal)


def smooth_once(padded, right_side, weights, keep_mask):
    west_face, east_face, outer_face, inner_face, diagonal, gain_step = weights
    centre = padded[:, 1:-1]
    edge_zeros = jnp.zeros_like(centre[..., :1])
    upward = jnp.concatenate([centre[..., 1:], edge_zeros], axis=-1)
    downward = jnp.concatenate([edge_zeros, centre[..., :-1]], axis=-1)
    applied = (
        diagonal * centre
        - west_face * padded[:, :-2]
        - east_face * padded[:, 2:]
        - outer_face * upward
        - inner_face * downward
    )
    return keep_mask * (centre + gain_step * (right_side - applied))


def body(adjoint_end, adjoint_source, region, dirichlet, reluctivity, conductance):
    columns = adjoint_end.shape[1]
    radial = adjoint_end.shape[2]
    steps = adjoint_source.shape[1]
    spacing = 2.0 * math.pi / (columns * lax.axis_size("space"))
    position = jnp.arange(radial, dtype=jnp.float32)
    reluct = lookup(region, reluctivity)
    mass_term = lookup(region, conductance) * (1.0 + position * spacing)
    keep_mask = (1 - dirichlet).astype(jnp.float32)
    reluct_pad = extended(reluct, (("space", 0),), 1)
    weights = face_weights(reluct_pad, mass_term, spacing)
    state = adjoint_end
    for step_index in range(steps):
        right_side = mass_term * state + adjoint_source[:, step_index]
        for sweep_index in range(SWEEPS):
            padded = extended(state, (("space", 1),), 1)
            state = smooth_once(padded, right_side, weights, keep_mask)
    passed = from_behind(state[0], "tm", -1)
    return jnp.concatenate([state[1:], passed[None]], axis=0)


def solution(mesh):
    return jax.shard_map(
        body,
        mesh=mesh,
        in_specs=(
            P("tm", "space", None),
            P("tm", None, "space", None),
            P("space", None),
            P("space", None),
            P(),
            P(),
        ),
        out_specs=P("tm", "space", None),
        check_vma=False,
    )
```

profile of v0, /device:TPU:1, one launch (start us, length us, event | category | flops | bytes accessed | tf_op | source)
XLA Modules:
  0.0 98.2 jit_solution(17593690496242766741)
XLA Ops:
  0.0 0.9 fusion.61
  0.9 3.7 %collective-permute-start.2 = (f32[2,1,1024]{2,1,0:T(1,128)S(1)}, f32[2,1,1024]{2,1,0:T(1,128)S(1)}, u32[]{:S(2)}, u32[]{:S(2)}) collective-permute-start(f32[2,1,1024]{2,1,0:T(1,128)S(1)} %get-tuple-element.36), channel_id=1, source_target_pairs={{0,1},{1,2},{2,3},{3,4},{4,5},{5,6},{6,7},{7,8},{8,9},{9,10},{10,1... | collective-permute-start | bytes 24584 | tf_op jit(solution)/shard_map/ppermute | solution.py:21
  4.5 7.8 %collective-permute-start.3 = (f32[2,1,1024]{2,1,0:T(1,128)S(1)}, f32[2,1,1024]{2,1,0:T(1,128)S(1)}, u32[]{:S(2)}, u32[]{:S(2)}) collective-permute-start(f32[2,1,1024]{2,1,0:T(1,128)S(1)} %get-tuple-element.37), channel_id=1, source_target_pairs={{1,0},{2,1},{3,2},{4,3},{5,4},{6,5},{7,6},{8,7},{9,8},{10,9},{11,1... | collective-permute-start | bytes 24584 | tf_op jit(solution)/shard_map/ppermute | solution.py:22
  12.4 1.6 %fusion.66 = (f32[1]{0:T(128)}, f32[1]{0:T(128)}, f32[1]{0:T(128)}, f32[1]{0:T(128)}, f32[1]{0:T(128)}, /*index=5*/f32[1]{0:T(128)}, f32[1]{0:T(128)}, f32[1]{0:T(128)}) fusion(f32[8]{0:T(128)} %param.10), kind=kLoop, calls=%fused_computation.93 | loop fusion | bytes 64 | tf_op jit(solution)/shard_map/slice | solution.py:35
  14.0 7.6 %select_select_fusion = (f32[256,1024]{1,0:T(8,128)S(1)}, pred[256,1024]{1,0:T(8,128)(4,1)S(1)}, pred[256,1024]{1,0:T(8,128)(4,1)S(1)}, pred[256,1024]{1,0:T(8,1...) fusion(f32[]{:T(128)} %bitcast.15, f32[]{:T(128)} %bitcast.14, ...), kind=kLoop, calls=%fused_computation.66 | loop fusion | flops 4194304 | bytes 4194336 | tf_op jit(solution)/shard_map/jit(_where)/select_n | solution.py:35
  21.6 3.0 %collective-permute-start.1 = (f32[1,1024]{1,0:T(1,128)S(1)}, f32[1,1024]{1,0:T(1,128)S(1)}, u32[]{:S(2)}, u32[]{:S(2)}) collective-permute-start(f32[1,1024]{1,0:T(1,128)S(1)} %get-tuple-element.42), channel_id=1, source_target_pairs={{1,0},{2,1},{3,2},{4,3},{5,4},{6,5},{7,6},{8,7},{9,8},{10,9},{11,1... | collective-permute-start | bytes 12296 | tf_op jit(solution)/shard_map/ppermute | solution.py:22
  24.6 0.1 collective-permute-start
  24.7 0.1 fusion.62
  24.8 0.0 copy-start
  24.8 0.4 fusion.63
  25.2 1.2 %copy-done = f32[2,256,1024]{2,1,0:T(8,128)S(1)} copy-done((f32[2,256,1024]{2,1,0:T(8,128)S(1)}, f32[2,256,1024]{2,1,0:T(8,128)}, u32[]{:S(2)}) %copy-start) | copy-done | bytes 2097176
  26.4 0.0 copy-start.3
  26.4 0.8 fusion.60
  27.2 0.0 copy-done.3
  27.2 0.7 fusion.65
  27.9 0.0 copy-done.2
  27.9 0.1 subtract_convert_fusion
  28.1 0.0 collective-permute-done.1
  28.1 4.7 %collective-permute-done = f32[1,1024]{1,0:T(1,128)S(1)} collective-permute-done((f32[1,1024]{1,0:T(1,128)S(1)}, f32[1,1024]{1,0:T(1,128)S(1)}, u32[]{:S(2)}, u32[]{:S(2)}) %collective-permute-start) | collective-permute-done | bytes 4128 | tf_op jit(solution)/shard_map/ppermute | solution.py:21
  32.8 7.2 %fusion.48 = (f32[256,1024]{1,0:T(8,128)S(1)}, f32[256,1024]{1,0:T(8,128)S(1)}, f32[256,1024]{1,0:T(8,128)S(1)}, f32[256,1024]{1,0:T(8,128)S(1)}, f32[256,1024]{1,0:T(8,128)S(1)}, /*index=5*/f32[256,1024]{1,0:T(8,128)S(1)}) fusion(f32[1024]{0:T(1024)S(1)} %multiply_add_fusion, pred[256,1024]{1,0:T(8,128)(4,1)S(1)} %get-tuple-element.19, ...), kind=kLoop, calls=%fused_computation.65 | loop fusion | flops 7340032 | bytes 11554848 | tf_op jit(solution)/shard_map/div | solution.py:53
  40.0 0.0 copy-start.1
  40.0 0.6 add_add_fusion
  40.6 0.0 collective-permute-done.2
  40.6 0.0 collective-permute-done.3
  40.6 1.5 %copy-done.1 = f32[2,2,256,1024]{3,2,1,0:T(8,128)S(1)} copy-done((f32[2,2,256,1024]{3,2,1,0:T(8,128)S(1)}, f32[2,2,256,1024]{3,2,1,0:T(8,128)}, u32[]{:S(2)}) %copy-start.1) | copy-done | bytes 4194328
  42.1 2.4 %fusion.37 = f32[2,256,1024]{2,1,0:T(8,128)S(1)} fusion(f32[2,256,1024]{2,1,0:T(8,128)S(1)} %copy-done, f32[2,1,1024]{2,1,0:T(1,128)S(1)} %collective-permute-done.3, f32[2,1,1024]{2,1,0:T(1,128)S(1)} %collective-permute-done.2, f32[2,256,1023]{2,1,0:T(8,128)S(1)} %get-tuple-element.35, f32[2,256,1023]{2,1,0:T(8,128)S(1)} %get-tuple-element.34, ...), kind=kLoop, calls=%fused_computation.44 | loop fusion | flops 8912896 | bytes 18886656 | tf_op jit(solution)/shard_map/mul | solution.py:69
  44.5 0.1 collective-permute-start.4
  44.6 7.2 %collective-permute-start.5 = (f32[2,1,1024]{2,1,0:T(1,128)S(1)}, f32[2,1,1024]{2,1,0:T(1,128)S(1)}, u32[]{:S(2)}, u32[]{:S(2)}) collective-permute-start(f32[2,1,1024]{2,1,0:T(1,128)S(1)} %get-tuple-element.33), channel_id=1, source_target_pairs={{1,0},{2,1},{3,2},{4,3},{5,4},{6,5},{7,6},{8,7},{9,8},{10,9},{11,1... | collective-permute-start | bytes 24584 | tf_op jit(solution)/shard_map/ppermute | solution.py:22
  51.8 0.8 fusion.58
  52.6 0.2 collective-permute-done.4
  52.8 0.0 collective-permute-done.5
  52.8 2.8 %fusion.27 = f32[2,256,1024]{2,1,0:T(8,128)S(1)} fusion(f32[2,256,1024]{2,1,0:T(8,128)S(1)} %fusion.37, f32[2,1,1024]{2,1,0:T(1,128)S(1)} %collective-permute-done.5, f32[2,1,1024]{2,1,0:T(1,128)S(1)} %collective-permute-done.4, f32[2,256,1023]{2,1,0:T(8,128)S(1)} %get-tuple-element.31, f32[2,256,1023]{2,1,0:T(8,128)S(1)} %get-tuple-element.30, ...), kind=kLoop, calls=%fused_computation.32 | loop fusion | flops 8912896 | bytes 20983808 | tf_op jit(solution)/shard_map/mul | solution.py:69
  55.7 0.1 collective-permute-start.6
  55.8 7.3 %collective-permute-start.7 = (f32[2,1,1024]{2,1,0:T(1,128)S(1)}, f32[2,1,1024]{2,1,0:T(1,128)S(1)}, u32[]{:S(2)}, u32[]{:S(2)}) collective-permute-start(f32[2,1,1024]{2,1,0:T(1,128)S(1)} %get-tuple-element.29), channel_id=1, source_target_pairs={{1,0},{2,1},{3,2},{4,3},{5,4},{6,5},{7,6},{8,7},{9,8},{10,9},{11,1... | collective-permute-start | bytes 24584 | tf_op jit(solution)/shard_map/ppermute | solution.py:22
  63.0 0.8 fusion.56
  63.9 0.1 collective-permute-done.6
  64.0 0.0 collective-permute-done.7
  64.0 2.5 %fusion.17 = f32[2,256,1024]{2,1,0:T(8,128)S(1)} fusion(f32[2,256,1024]{2,1,0:T(8,128)S(1)} %fusion.27, f32[2,1,1024]{2,1,0:T(1,128)S(1)} %collective-permute-done.7, f32[2,1,1024]{2,1,0:T(1,128)S(1)} %collective-permute-done.6, f32[2,256,1023]{2,1,0:T(8,128)S(1)} %get-tuple-element.27, f32[2,256,1023]{2,1,0:T(8,128)S(1)} %get-tuple-element.26, ...), kind=kLoop, calls=%fused_computation.20 | loop fusion | flops 8912896 | bytes 18886656 | tf_op jit(solution)/shard_map/mul | solution.py:69
  66.5 0.1 collective-permute-start.8
  66.6 7.3 %collective-permute-start.9 = (f32[2,1,1024]{2,1,0:T(1,128)S(1)}, f32[2,1,1024]{2,1,0:T(1,128)S(1)}, u32[]{:S(2)}, u32[]{:S(2)}) collective-permute-start(f32[2,1,1024]{2,1,0:T(1,128)S(1)} %get-tuple-element.25), channel_id=1, source_target_pairs={{1,0},{2,1},{3,2},{4,3},{5,4},{6,5},{7,6},{8,7},{9,8},{10,9},{11,1... | collective-permute-start | bytes 24584 | tf_op jit(solution)/shard_map/ppermute | solution.py:22
  74.0 0.8 fusion.54
  74.8 0.1 collective-permute-done.8
  74.9 0.0 collective-permute-done.9
  74.9 2.8 %fusion.7 = f32[2,256,1024]{2,1,0:T(8,128)S(1)} fusion(f32[2,256,1024]{2,1,0:T(8,128)S(1)} %fusion.17, f32[2,1,1024]{2,1,0:T(1,128)S(1)} %collective-permute-done.9, f32[2,1,1024]{2,1,0:T(1,128)S(1)} %collective-permute-done.8, f32[2,256,1023]{2,1,0:T(8,128)S(1)} %get-tuple-element.23, f32[2,256,1023]{2,1,0:T(8,128)S(1)} %get-tuple-element.22, ...), kind=kLoop, calls=%fused_computation.8 | loop fusion | flops 8912896 | bytes 20983808 | tf_op jit(solution)/shard_map/mul | solution.py:69
  77.7 0.1 fusion.53
  77.9 6.2 %collective-permute-start.10 = (f32[256,1024]{1,0:T(8,128)S(1)}, f32[256,1024]{1,0:T(8,128)S(1)}, u32[]{:S(2)}, u32[]{:S(2)}) collective-permute-start(f32[256,1024]{1,0:T(8,128)S(1)} %get-tuple-element.21), channel_id=1, source_target_pairs={{0,192},{64,0},{128,64},{192,128},{1,193},{65,1},{129,65},{193,129... | collective-permute-start | bytes 3145736 | tf_op jit(solution)/shard_map/ppermute | solution.py:29
  84.1 12.7 %collective-permute-done.10 = f32[256,1024]{1,0:T(8,128)S(1)} collective-permute-done((f32[256,1024]{1,0:T(8,128)S(1)}, f32[256,1024]{1,0:T(8,128)S(1)}, u32[]{:S(2)}, u32[]{:S(2)}) %collective-permute-start.10) | collective-permute-done | bytes 1048608 | tf_op jit(solution)/shard_map/ppermute | solution.py:29
  96.7 1.5 %pad_maximum_fusion.8 = f32[2,256,1024]{2,1,0:T(8,128)} fusion(f32[1,256,1024]{2,1,0:T(8,128)S(1)} %bitcast.35, f32[1,256,1024]{2,1,0:T(8,128)S(1)} %get-tuple-element.20), kind=kLoop, calls=%fused_computation.48 | loop fusion | flops 524288 | bytes 4194304 | tf_op jit(solution)/shard_map/concatenate | solution.py:90
  (7 shorter events, 0.1 us)
Async XLA Ops:
  0.9 39.7 %collective-permute-start.2 = (f32[2,1,1024]{2,1,0:T(1,128)S(1)}, f32[2,1,1024]{2,1,0:T(1,128)S(1)}, u32[]{:S(2)}, u32[]{:S(2)}) collective-permute-start(f32[2,1,1024]{2,1,0:T(1,128)S(1)} %get-tuple-element.36), channel_id=1, source_target_pairs={{0,1},{1,2},{2,3},{3,4},{4,5},{5,6},{6,7},{7,8},{8,9},{9,10},{10,1... | collective-permute-start | bytes 24584 | tf_op jit(solution)/shard_map/ppermute | solution.py:21
  4.5 36.1 %collective-permute-start.3 = (f32[2,1,1024]{2,1,0:T(1,128)S(1)}, f32[2,1,1024]{2,1,0:T(1,128)S(1)}, u32[]{:S(2)}, u32[]{:S(2)}) collective-permute-start(f32[2,1,1024]{2,1,0:T(1,128)S(1)} %get-tuple-element.37), channel_id=1, source_target_pairs={{1,0},{2,1},{3,2},{4,3},{5,4},{6,5},{7,6},{8,7},{9,8},{10,9},{11,1... | collective-permute-start | bytes 24584 | tf_op jit(solution)/shard_map/ppermute | solution.py:22
  21.6 6.5 %collective-permute-start.1 = (f32[1,1024]{1,0:T(1,128)S(1)}, f32[1,1024]{1,0:T(1,128)S(1)}, u32[]{:S(2)}, u32[]{:S(2)}) collective-permute-start(f32[1,1024]{1,0:T(1,128)S(1)} %get-tuple-element.42), channel_id=1, source_target_pairs={{1,0},{2,1},{3,2},{4,3},{5,4},{6,5},{7,6},{8,7},{9,8},{10,9},{11,1... | collective-permute-start | bytes 12296 | tf_op jit(solution)/shard_map/ppermute | solution.py:22
  24.6 8.2 %collective-permute-start = (f32[1,1024]{1,0:T(1,128)S(1)}, f32[1,1024]{1,0:T(1,128)S(1)}, u32[]{:S(2)}, u32[]{:S(2)}) collective-permute-start(f32[1,1024]{1,0:T(1,128)S(1)} %get-tuple-element.43), channel_id=1, source_target_pairs={{0,1},{1,2},{2,3},{3,4},{4,5},{5,6},{6,7},{7,8},{8,9},{9,10},{10,1... | collective-permute-start | bytes 12296 | tf_op jit(solution)/shard_map/ppermute | solution.py:21
  24.8 1.6 %copy-start = (f32[2,256,1024]{2,1,0:T(8,128)S(1)}, f32[2,256,1024]{2,1,0:T(8,128)}, u32[]{:S(2)}) copy-start(f32[2,256,1024]{2,1,0:T(8,128)} %param.6) | copy-start | bytes 6291460
  26.4 0.8 copy-start.3
  26.4 1.5 %copy-start.2 = (s32[256,1024]{1,0:T(8,128)S(1)}, s32[256,1024]{1,0:T(8,128)}, u32[]{:S(2)}) copy-start(s32[256,1024]{1,0:T(8,128)} %param.9) | copy-start | bytes 3145732
  40.0 2.2 %copy-start.1 = (f32[2,2,256,1024]{3,2,1,0:T(8,128)S(1)}, f32[2,2,256,1024]{3,2,1,0:T(8,128)}, u32[]{:S(2)}) copy-start(f32[2,2,256,1024]{3,2,1,0:T(8,128)} %param.7) | copy-start | bytes 12582916
  44.5 8.3 %collective-permute-start.4 = (f32[2,1,1024]{2,1,0:T(1,128)S(1)}, f32[2,1,1024]{2,1,0:T(1,128)S(1)}, u32[]{:S(2)}, u32[]{:S(2)}) collective-permute-start(f32[2,1,1024]{2,1,0:T(1,128)S(1)} %get-tuple-element.32), channel_id=1, source_target_pairs={{0,1},{1,2},{2,3},{3,4},{4,5},{5,6},{6,7},{7,8},{8,9},{9,10},{10,1... | collective-permute-start | bytes 24584 | tf_op jit(solution)/shard_map/ppermute | solution.py:21
  44.6 8.2 %collective-permute-start.5 = (f32[2,1,1024]{2,1,0:T(1,128)S(1)}, f32[2,1,1024]{2,1,0:T(1,128)S(1)}, u32[]{:S(2)}, u32[]{:S(2)}) collective-permute-start(f32[2,1,1024]{2,1,0:T(1,128)S(1)} %get-tuple-element.33), channel_id=1, source_target_pairs={{1,0},{2,1},{3,2},{4,3},{5,4},{6,5},{7,6},{8,7},{9,8},{10,9},{11,1... | collective-permute-start | bytes 24584 | tf_op jit(solution)/shard_map/ppermute | solution.py:22
  55.7 8.3 %collective-permute-start.6 = (f32[2,1,1024]{2,1,0:T(1,128)S(1)}, f32[2,1,1024]{2,1,0:T(1,128)S(1)}, u32[]{:S(2)}, u32[]{:S(2)}) collective-permute-start(f32[2,1,1024]{2,1,0:T(1,128)S(1)} %get-tuple-element.28), channel_id=1, source_target_pairs={{0,1},{1,2},{2,3},{3,4},{4,5},{5,6},{6,7},{7,8},{8,9},{9,10},{10,1... | collective-permute-start | bytes 24584 | tf_op jit(solution)/shard_map/ppermute | solution.py:21
  55.8 8.2 %collective-permute-start.7 = (f32[2,1,1024]{2,1,0:T(1,128)S(1)}, f32[2,1,1024]{2,1,0:T(1,128)S(1)}, u32[]{:S(2)}, u32[]{:S(2)}) collective-permute-start(f32[2,1,1024]{2,1,0:T(1,128)S(1)} %get-tuple-element.29), channel_id=1, source_target_pairs={{1,0},{2,1},{3,2},{4,3},{5,4},{6,5},{7,6},{8,7},{9,8},{10,9},{11,1... | collective-permute-start | bytes 24584 | tf_op jit(solution)/shard_map/ppermute | solution.py:22
  66.5 8.4 %collective-permute-start.8 = (f32[2,1,1024]{2,1,0:T(1,128)S(1)}, f32[2,1,1024]{2,1,0:T(1,128)S(1)}, u32[]{:S(2)}, u32[]{:S(2)}) collective-permute-start(f32[2,1,1024]{2,1,0:T(1,128)S(1)} %get-tuple-element.24), channel_id=1, source_target_pairs={{0,1},{1,2},{2,3},{3,4},{4,5},{5,6},{6,7},{7,8},{8,9},{9,10},{10,1... | collective-permute-start | bytes 24584 | tf_op jit(solution)/shard_map/ppermute | solution.py:21
  66.6 8.3 %collective-permute-start.9 = (f32[2,1,1024]{2,1,0:T(1,128)S(1)}, f32[2,1,1024]{2,1,0:T(1,128)S(1)}, u32[]{:S(2)}, u32[]{:S(2)}) collective-permute-start(f32[2,1,1024]{2,1,0:T(1,128)S(1)} %get-tuple-element.25), channel_id=1, source_target_pairs={{1,0},{2,1},{3,2},{4,3},{5,4},{6,5},{7,6},{8,7},{9,8},{10,9},{11,1... | collective-permute-start | bytes 24584 | tf_op jit(solution)/shard_map/ppermute | solution.py:22
  77.9 18.9 %collective-permute-start.10 = (f32[256,1024]{1,0:T(8,128)S(1)}, f32[256,1024]{1,0:T(8,128)S(1)}, u32[]{:S(2)}, u32[]{:S(2)}) collective-permute-start(f32[256,1024]{1,0:T(8,128)S(1)} %get-tuple-element.21), channel_id=1, source_target_pairs={{0,192},{64,0},{128,64},{192,128},{1,193},{65,1},{129,65},{193,129... | collective-permute-start | bytes 3145736 | tf_op jit(solution)/shard_map/ppermute | solution.py:29
where the time goes:
time: 98.6 us; the launch traced here: 98.2 us
  starting transfers between devices  42.8 us (43%)
  other arithmetic  27.5 us (28%)
  waiting for transfers between devices  17.8 us (18%)
  local copies, waits for them, and re-layouts  9.92 us (10%)
    ppermute x5, starting transfers between devices, extended(): after = lax.ppermute(leading, axis, down)  32.6 us
    ppermute x1, waiting for transfers between devices, from_behind(): lax.ppermute(shard, axis, [(i, (i + by) % devices) for i in range(devices)])  12.7 us
    mul x4, other arithmetic, smooth_once(): return keep_mask * (centre + gain_step * (right_side - applied))  10.5 us
    select_n x1, other arithmetic, lookup(): result = jnp.where(region == entry, table[entry], result)  7.62 us
    div x1, other arithmetic, face_weights(): relaxation / diagonal  7.17 us
    ppermute x1, starting transfers between devices, from_behind(): lax.ppermute(shard, axis, [(i, (i + by) % devices) for i in range(devices)])  6.19 us
    ppermute x5, waiting for transfers between devices, extended(): before = lax.ppermute(last, axis, up)  5.1 us
    ppermute x5, starting transfers between devices, extended(): before = lax.ppermute(last, axis, up)  3.99 us
  transfers between devices with their start and end apart: 11, of which 5 were waited for; matrix products, arithmetic and copies ran while one was open for 22% of the time, Pallas kernels for 0%

commit v1 on v0

v1 whole, which is shorter than its diff:
```python
import functools
import math

import jax
import jax.numpy as jnp
from jax import lax
from jax.experimental import pallas as pl
from jax.experimental.pallas import tpu as pltpu
from jax.sharding import PartitionSpec as P

RELAX = 0.8
KEEP_SHARE = 0.2
F32 = jnp.float32
ANY = pl.BlockSpec(memory_space=pltpu.HBM)
VMEM = pl.BlockSpec(memory_space=pltpu.VMEM)
SMEM = pl.BlockSpec(memory_space=pltpu.SMEM)
PLANES = 7
LOOK, MAKE, GO = 9, 3, 9


def tables(region, *names):
    low = (region & 1) != 0
    mid = (region & 2) != 0
    top = (region & 4) != 0
    found = []
    for t in names:
        pairs = [jnp.where(low, t[2 * k + 1], t[2 * k]) for k in range(4)]
        halves = [jnp.where(mid, pairs[2 * k + 1], pairs[2 * k]) for k in range(2)]
        found.append(jnp.where(top, halves[1], halves[0]))
    return found


def row_factors(rows, radial, spacing):
    lane = lax.broadcasted_iota(jnp.int32, (rows, radial), 1)
    position = lane.astype(F32)
    cycle = 1.0 + position * spacing
    outer = 0.5 * (1.0 + (position + 0.5) * spacing)
    inner = 0.5 * (1.0 + (position - 0.5) * spacing)
    return lane, cycle, 0.5 / cycle, outer, inner


def weight_planes(rho, rho_west, rho_east, cond, dirichlet, factors):
    lane, cycle, half_cycle, outer_f, inner_f = factors
    radial = rho.shape[1]
    first, final = lane == 0, lane == radial - 1
    up = jnp.where(final, rho, pltpu.roll(rho, radial - 1, 1))
    down = jnp.where(first, rho, pltpu.roll(rho, 1, 1))
    west = (rho + rho_west) * half_cycle
    east = (rho + rho_east) * half_cycle
    outer = (rho + up) * outer_f
    inner = (rho + down) * inner_f
    mass = cond * cycle
    diagonal = mass + west + east + outer + inner
    free = dirichlet == 0
    gain = jnp.where(free, RELAX / diagonal, 0.0)
    own = jnp.where(free, KEEP_SHARE, 0.0)
    outer_gain = jnp.where(final, 0.0, gain * outer)
    inner_gain = jnp.where(first, 0.0, gain * inner)
    return own, gain * west, gain * east, outer_gain, inner_gain, gain, gain * mass


def stencil(centre, west, east, w, right):
    radial = centre.shape[1]
    up = pltpu.roll(centre, radial - 1, 1)
    down = pltpu.roll(centre, 1, 1)
    return (w[0] * centre + w[1] * west) + (w[2] * east + w[3] * up) + (w[4] * down + right)


def copy_in(src, dst, sem):
    return pltpu.make_async_copy(src, dst, sem)


def each(lo, hi, work, group):
    group = min(group, hi - lo)
    groups = -(-(hi - lo) // group)

    def step(k, _):
        at = jnp.minimum(lo + k * group, hi - group)
        work([at + m for m in range(group)])
        return 0

    lax.fori_loop(0, groups, step, 0)


def beside(x, t, sub):
    c = x[t + 1]
    west = jnp.where(sub == 0, x[t, 7:8, :], pltpu.roll(c, 1, 0))
    east = jnp.where(sub == 7, x[t + 2, 0:1, :], pltpu.roll(c, 7, 0))
    return c, west, east


def weights_loop(reg, diri, rho_s, cond_s, fac, w_out, rho_tab, cond_tab, tiles):
    radial = reg.shape[2]

    def look(ts):
        found = [tables(reg[t], rho_tab, cond_tab) for t in ts]
        for t, (r, c) in zip(ts, found):
            rho_s[t + 1] = r
            cond_s[t] = c

    each(0, tiles, look, LOOK)
    lane = lax.broadcasted_iota(jnp.int32, (8, radial), 1)
    sub = lax.broadcasted_iota(jnp.int32, (8, radial), 0)

    def make(ts):
        seen = [beside(rho_s, t, sub) + (cond_s[t], diri[t]) for t in ts]
        planes = [weight_planes(*v, (lane, fac[0], fac[1], fac[2], fac[3])) for v in seen]
        for t, w in zip(ts, planes):
            for k in range(PLANES):
                w_out[k, t] = w[k]

    each(0, tiles, make, MAKE)


def sweep(x, y, w, w_at, src, right, first, lo, hi, y_at=1):
    sub = lax.broadcasted_iota(jnp.int32, x.shape[1:], 0)

    def go(ts):
        seen = [beside(x, t, sub) for t in ts]
        rights, news = [], []
        for t, (c, west, east) in zip(ts, seen):
            if first:
                b = w[5, t - w_at] * src[t] + w[6, t - w_at] * c
            else:
                b = right[t]
            rights.append(b)
            news.append(stencil(c, west, east, [w[k, t - w_at] for k in range(5)], b))
        for t, b, new in zip(ts, rights, news):
            if first:
                right[t] = b
            y[t + y_at] = new

    each(lo, hi, go, GO)


def edge_loads(end, source, region, diri, at, buf, regs, sems):
    return [
        copy_in(end.at[1, at], buf.at[0], sems.at[0]),
        copy_in(source.at[1, 0, at], buf.at[1], sems.at[1]),
        copy_in(source.at[1, 1, at], buf.at[2], sems.at[2]),
        copy_in(end.at[0, at], buf.at[3], sems.at[3]),
        copy_in(source.at[0, 0, at], buf.at[4], sems.at[4]),
        copy_in(source.at[0, 1, at], buf.at[5], sems.at[5]),
        copy_in(region.at[at], regs.at[0], sems.at[6]),
        copy_in(diri.at[at], regs.at[1], sems.at[7]),
    ]


def write_packs(buf, regs, a, b, side):
    pick = (lambda m: slice(0, m)) if side == 0 else (lambda m: slice(8 - m, 8))
    for out, at in ((a, 0), (b, 3)):
        out[0:4, :] = buf[at, pick(4), :]
        out[4:7, :] = buf[at + 1, pick(3), :]
        out[7:8, :] = buf[at + 2, pick(1), :]
    a[8:12, :] = regs[0, pick(4), :].astype(F32)
    a[12:15, :] = regs[1, pick(3), :].astype(F32)
    a[15:16, :] = jnp.zeros((1, a.shape[1]), F32)


def pack_kernel(end, source, region, diri, up_a, up_b, own, buf, regs, sems):
    last = end.shape[1] - 1
    copies = edge_loads(end, source, region, diri, last, buf, regs, sems)
    copies += [
        copy_in(end.at[0, 0], own.at[0], sems.at[8]),
        copy_in(source.at[0, 0, 0], own.at[1], sems.at[9]),
        copy_in(source.at[0, 1, 0], own.at[2], sems.at[10]),
    ]
    for c in copies:
        c.start()
    for c in copies:
        c.wait()
    write_packs(buf, regs, up_a, up_b, 1)
    for k in range(3):
        own[3 + k] = buf[3 + k]


def chunk_kernel(base, tiles, lo, hi, spacing, rho_tab, cond_tab, end, source, region, diri, _, *refs):
    w_out, chunk = refs[:2]
    packs = refs[2:-13]
    reg_v, dir_v, x, y, s0, s1, right, rho_s, cond_s, fac, rt, ct, sems = refs[-13:]
    if packs:
        *packs, buf, regs, edge_sems = packs
    radial = end.shape[3]
    rows = pl.ds(base, tiles)
    copies = [
        copy_in(rho_tab, rt, sems.at[0]),
        copy_in(cond_tab, ct, sems.at[1]),
        copy_in(region.at[rows], reg_v, sems.at[2]),
        copy_in(diri.at[rows], dir_v, sems.at[3]),
        copy_in(end.at[0, rows], x.at[pl.ds(1, tiles)], sems.at[4]),
        copy_in(source.at[0, 0, rows], s0, sems.at[5]),
        copy_in(source.at[0, 1, rows], s1, sems.at[6]),
    ]
    for c in copies:
        c.start()
    if packs:
        edges = edge_loads(end, source, region, diri, 0, buf, regs, edge_sems)
        for c in edges:
            c.start()
    _, cycle, half, outer, inner = row_factors(8, radial, spacing)
    for k, f in enumerate((cycle, half, outer, inner)):
        fac[k] = f
    for c in copies[:4]:
        c.wait()
    rts = [rt[k] for k in range(8)]
    cts = [ct[k] for k in range(8)]
    weights_loop(reg_v, dir_v, rho_s, cond_s, fac, w_out, rts, cts, tiles)
    copies[4].wait()
    copies[5].wait()
    sweep(x, y, w_out, 0, s0, right, True, 0, tiles)
    sweep(y, x, w_out, 0, None, right, False, 0, tiles)
    copies[6].wait()
    sweep(x, y, w_out, 0, s1, right, True, 0, tiles)
    sweep(y, chunk, w_out, 0, None, right, False, lo, hi, -lo)
    if packs:
        for c in edges:
            c.wait()
        write_packs(buf, regs, packs[0], packs[1], 0)


def second_kernel(w1, w2, end, source, out, ends, x, y, s0, s1, right, sems):
    tiles = end.shape[1]
    half = tiles // 2
    quarter = tiles // 4

    def piece(k):
        return pl.ds(k * quarter, quarter)

    def load(k):
        return [
            copy_in(end.at[1, piece(k)], x.at[pl.ds(1 + k * quarter, quarter)], sems.at[0, k]),
            copy_in(source.at[1, 0, piece(k)], s0.at[piece(k)], sems.at[1, k]),
        ]

    def back(k):
        return copy_in(x.at[pl.ds(1 + k * quarter, quarter)], out.at[0, piece(k)], sems.at[2, k])

    late = copy_in(source.at[1, 1], s1, sems.at[3, 0])
    for k in range(4):
        for c in load(k):
            c.start()
    late.start()
    skip = tiles - w2.shape[1]

    def both(a, b, src, first, before=None, after=None):
        for k in range(4):
            if before:
                before(k)
            w, at = (w1, 0) if k < 2 else (w2, skip)
            sweep(a, b, w, at, src, right, first, k * quarter, (k + 1) * quarter)
            if after:
                after(k)

    def arrived(k):
        for p in ([0, 1] if k == 0 else [k + 1] if k < 3 else []):
            for c in load(p):
                c.wait()

    both(x, y, s0, True, arrived)
    both(y, x, None, False)
    late.wait()
    both(x, y, s1, True)
    both(y, x, None, False, None, lambda k: back(k).start())
    ends[0] = x[1]
    ends[1] = x[tiles]
    for k in range(4):
        back(k).wait()


def edge_kernel(
    side, spacing,
    rho_tab, cond_tab, end, source, region, diri, got, bulk, ends, pa, pb, _,
    out,
    own, regs, xw, sw, rw, dw, tiles_out, rt, ct, sems,
):
    tiles, radial = end.shape[1], end.shape[3]
    half = tiles // 2
    at = side * (tiles - 1)
    moved = copy_in(
        bulk.at[pl.ds(1 - side, half - 1)], out.at[1, pl.ds(1 if side == 0 else half, half - 1)], sems.at[0]
    )
    loads = [
        copy_in(rho_tab, rt, sems.at[1]),
        copy_in(cond_tab, ct, sems.at[2]),
        copy_in(region.at[at], regs.at[0], sems.at[3]),
        copy_in(diri.at[at], regs.at[1], sems.at[4]),
        copy_in(end.at[1, at], own.at[0], sems.at[5]),
        copy_in(source.at[1, 0, at], own.at[1], sems.at[6]),
        copy_in(source.at[1, 1, at], own.at[2], sems.at[7]),
    ]
    for c in loads:
        c.start()
    moved.start()
    factors = row_factors(16, radial, spacing)
    zero = jnp.zeros((16, radial), F32)
    mine = 8 if side == 0 else 0
    halo = (lambda m: slice(8 - m, 8)) if side == 0 else (lambda m: slice(8, 8 + m))
    rw[...] = jnp.zeros((16, radial), jnp.int32)
    dw[...] = jnp.zeros((16, radial), jnp.int32)
    rw[halo(4), :] = pa[8:12, :].astype(jnp.int32)
    dw[halo(3), :] = pa[12:15, :].astype(jnp.int32)
    for p, pack in ((0, pa), (1, pb)):
        xw[p] = zero
        sw[p, 0] = zero
        sw[p, 1] = zero
        xw[p, halo(4), :] = pack[0:4, :]
        sw[p, 0, halo(3), :] = pack[4:7, :]
        sw[p, 1, halo(1), :] = pack[7:8, :]
    xw[1, mine : mine + 8, :] = got[3 * side]
    sw[1, 0, mine : mine + 8, :] = got[3 * side + 1]
    sw[1, 1, mine : mine + 8, :] = got[3 * side + 2]
    for c in loads:
        c.wait()
    rw[mine : mine + 8, :] = regs[0]
    dw[mine : mine + 8, :] = regs[1]
    xw[0, mine : mine + 8, :] = own[0]
    sw[0, 0, mine : mine + 8, :] = own[1]
    sw[0, 1, mine : mine + 8, :] = own[2]
    rho, cond = tables(rw[...], [rt[k] for k in range(8)], [ct[k] for k in range(8)])
    w = weight_planes(rho, pltpu.roll(rho, 1, 0), pltpu.roll(rho, 15, 0), cond, dw[...], factors)
    state = [xw[0], xw[1]]
    for step in range(2):
        right = [w[5] * sw[p, step] + w[6] * state[p] for p in range(2)]
        for _ in range(2):
            state = [
                stencil(v, pltpu.roll(v, 1, 0), pltpu.roll(v, 15, 0), w, r) for v, r in zip(state, right)
            ]
    sub = lax.broadcasted_iota(jnp.int32, (8, radial), 0)
    edge = sub < 4 if side == 0 else sub >= 4
    stores = []
    for p, keep in ((0, ends[side]), (1, bulk[side * (half - 1)])):
        tiles_out[p] = jnp.where(edge, state[p][mine : mine + 8, :], keep)
        stores.append(copy_in(tiles_out.at[p], out.at[p, at], sems.at[8 + p]))
        stores[-1].start()
    for c in [moved] + stores:
        c.wait()


def params(mib):
    return pltpu.CompilerParams(vmem_limit_bytes=mib * 2**20)


def cost(us):
    return pl.CostEstimate(flops=int(us * 4e3), bytes_accessed=int(us * 3e3), transcendentals=0)


def body(end, source, region, diri, rho_tab, cond_tab):
    n, radial = end.shape[1], end.shape[2]
    devices, rings = lax.axis_size("space"), lax.axis_size("tm")
    spacing = 2.0 * math.pi / (n * devices)
    tiles = n // 8
    part = tiles // 2 + 1

    end = end.reshape(2, tiles, 8, radial)
    source = source.reshape(2, 2, tiles, 8, radial)
    region = region.reshape(tiles, 8, radial)
    diri = diri.reshape(tiles, 8, radial)

    def f(*shape):
        return jax.ShapeDtypeStruct(shape + (radial,), F32)

    def buf(*shape):
        return pltpu.VMEM(shape + (radial,), F32)

    dma = pltpu.SemaphoreType.DMA
    ints = lambda *shape: pltpu.VMEM(shape + (radial,), jnp.int32)
    held = [pltpu.with_memory_space_constraint(v, pltpu.HBM) for v in (end, source, region, diri)]
    tabs = [pltpu.with_memory_space_constraint(v, pltpu.HBM) for v in (rho_tab, cond_tab)]
    tab_s = [pltpu.SMEM((rho_tab.shape[0],), F32)] * 2
    pack_a, pack_b, own = pl.pallas_call(
        pack_kernel,
        name="pack",
        out_shape=[f(16), f(8), f(6, 8)],
        in_specs=[ANY] * 4,
        out_specs=[VMEM] * 3,
        scratch_shapes=[buf(6, 8), ints(2, 8), dma((11,))],
        compiler_params=params(16),
        cost_estimate=cost(1.0),
    )(*held)

    up = [(t * devices + s, t * devices + (s + 1) % devices) for t in range(rings) for s in range(devices)]
    dn = [(b, a) for a, b in up]
    cross = lambda pairs: [(((a // devices + 1) % rings) * devices + a % devices, b) for a, b in pairs]
    both = ("tm", "space")
    back = [((t + 1) % rings, t) for t in range(rings)]
    got = lax.ppermute(own, "tm", back)
    up_a = lax.ppermute(pack_a, both, up)
    up_b = lax.ppermute(pack_b, both, cross(up))

    def chunk(base, lo, hi, after, packing):
        extra = [f(16), f(8)] if packing else []
        edge_s = [buf(6, 8), ints(2, 8), dma((8,))] if packing else []
        return pl.pallas_call(
            functools.partial(chunk_kernel, base, part, lo, hi, spacing),
            name="chunk",
            out_shape=[pltpu.VMEM((PLANES, part, 8, radial), F32), f(hi - lo, 8)] + extra,
            in_specs=[ANY] * 6 + [pl.BlockSpec(memory_space=pl.ANY)],
            out_specs=[VMEM] * (2 + len(extra)),
            scratch_shapes=edge_s + [
                ints(part, 8), ints(part, 8), buf(part + 2, 8), buf(part + 2, 8), buf(part, 8), buf(part, 8),
                buf(part, 8), buf(part + 2, 8), buf(part, 8), buf(4, 8),
            ] + tab_s + [dma((7,))],
            compiler_params=params(20),
            cost_estimate=cost(0.5),
        )(*tabs, *held, after)

    w1, c1 = chunk(0, 0, part - 1, own, False)
    w2, c2, dn_a, dn_b = chunk(tiles - part, 1, part, c1, True)
    c1 = lax.ppermute(c1, "tm", back)
    c2 = lax.ppermute(c2, "tm", back)
    dn_a = lax.ppermute(dn_a, both, dn)
    dn_b = lax.ppermute(dn_b, both, cross(dn))

    out, ends = pl.pallas_call(
        second_kernel,
        name="second",
        out_shape=[f(2, tiles, 8), f(2, 8)],
        in_specs=[VMEM, VMEM, ANY, ANY],
        out_specs=[ANY, VMEM],
        scratch_shapes=[buf(tiles + 2, 8)] * 2 + [buf(tiles, 8)] * 3 + [dma((4, 4))],
        compiler_params=params(20),
        cost_estimate=cost(0.5),
    )(w1, w2, *held[:2])

    for side, bulk, pa, pb in ((0, c1, up_a, up_b), (1, c2, dn_a, dn_b)):
        out = pl.pallas_call(
            functools.partial(edge_kernel, side, spacing),
            name="edge",
            out_shape=f(2, tiles, 8),
            in_specs=[ANY] * 6 + [VMEM] * 5 + [ANY],
            out_specs=ANY,
            scratch_shapes=[
                buf(3, 8), ints(2, 8), buf(2, 16), buf(2, 2, 16), ints(16), ints(16), buf(2, 8),
            ] + tab_s + [dma((10,))],
            input_output_aliases={11: 0},
            compiler_params=params(20),
            cost_estimate=cost(0.5),
        )(*tabs, *held, got, bulk, ends, pa, pb, out)
    return out.reshape(2, n, radial)


def solution(mesh):
    return jax.shard_map(
        body,
        mesh=mesh,
        in_specs=(
            P("tm", "space", None),
            P("tm", None, "space", None),
            P("space", None),
            P("space", None),
            P(),
            P(),
        ),
        out_specs=P("tm", "space", None),
        check_vma=False,
    )
```

time: 98.6 us -> 46.4 us (0.47)
  other arithmetic: 27.5 us -> 0 us
  starting transfers between devices: 42.8 us -> 17.2 us
  Pallas kernels: 0 us -> 19.8 us
  local copies, waits for them, and re-layouts: 9.92 us -> 0 us
  waiting for transfers between devices: 17.8 us -> 8.79 us
    ppermute x11 -> x7, starting transfers between devices: 42.8 us -> 17.2 us  [the longest x1 8.27 us: body(): dn_b = lax.ppermute(dn_b, both, cross(dn))]
    pallas_call x0 -> x6, Pallas kernels: none -> 19.8 us  [the longest x2 9.26 us: chunk(): pl.pallas_call(functools.partial(chunk_kernel, base, part, lo, hi, spacin...]
    mul x5 -> x0, other arithmetic: 10.5 us -> none  [the longest x4 10.5 us: smooth_once(): return keep_mask * (centre + gain_step * (right_side - applied))]
    ppermute x11 -> x7, waiting for transfers between devices: 17.8 us -> 8.79 us  [the longest x1 8.78 us: body(): up_b = lax.ppermute(pack_b, both, cross(up))]
    select_n x1 -> x0, other arithmetic: 7.62 us -> none  [lookup(): result = jnp.where(region == entry, table[entry], result)]
    slice x14 -> x0, local copies, waits for them, and re-layouts: 7.19 us -> none  [the longest x4 3.33 us: smooth_once(): upward = jnp.concatenate([centre[..., 1:], edge_zeros], axis=-1)]
    div x1 -> x0, other arithmetic: 7.17 us -> none  [face_weights(): relaxation / diagonal]
    unnamed x8 -> x0, local copies, waits for them, and re-layouts: 2.73 us -> none
  transfers between devices with their start and end apart: 11 -> 7, of which waited for: 5 -> 1; matrix products, arithmetic and copies ran while one was open for 22% -> 0% of each run, Pallas kernels for 0% -> 26%
where the time goes in v1:
time: 46.4 us; the launch traced here: 46 us
  Pallas kernels  19.8 us (43%)
  starting transfers between devices  17.2 us (37%)
  waiting for transfers between devices  8.79 us (19%)
    pallas_call x2, Pallas kernels, chunk(): pl.pallas_call(functools.partial(chunk_kernel, base, part, lo, hi, spacin...  9.26 us
    ppermute x1, waiting for transfers between devices, body(): up_b = lax.ppermute(pack_b, both, cross(up))  8.78 us
    ppermute x1, starting transfers between devices, body(): dn_b = lax.ppermute(dn_b, both, cross(dn))  8.27 us
    pallas_call x1, Pallas kernels, body(): pl.pallas_call(second_kernel, name='second', out_shape=[f(2, tiles, 8), f...  5.17 us
    pallas_call x2, Pallas kernels, body(): pl.pallas_call(functools.partial(edge_kernel, side, spacing), name='edge'...  4.32 us
    ppermute x1, starting transfers between devices, body(): c1 = lax.ppermute(c1, 'tm', back)  3.32 us
    ppermute x1, starting transfers between devices, body(): up_a = lax.ppermute(pack_a, both, up)  2.21 us
    ppermute x1, starting transfers between devices, body(): up_b = lax.ppermute(pack_b, both, cross(up))  1.79 us
  transfers between devices with their start and end apart: 7, of which 1 were waited for; matrix products, arithmetic and copies ran while one was open for 0% of the time, Pallas kernels for 26%

profile of v1, /device:TPU:1, one launch (start us, length us, event | category | flops | bytes accessed | tf_op | source)
XLA Modules:
  0.0 46.0 jit_solution(9464716610124424558)
XLA Ops:
  0.0 1.0 %pack.1 = (f32[16,1024]{1,0:T(8,128)S(1)}, f32[8,1024]{1,0:T(8,128)S(1)}, f32[6,8,1024]{2,1,0:T(8,128)S(1)}) custom-call(f32[2,32,8,1024]{3,2,1,0:T(8,128)} %bitcast.11, f32[2,2,32,8,1024]{4,3,2,1,0:T(8,128)} %bitcast.5, s32[32,8,1024]{2,1,0:T(8,128)} %bitcast.17, s32[32,8,1024]{2,1,0:T(8,128)} %bitcast.22), custom_call_target="tpu_custom_call" | custom-call | flops 4000 | bytes 3000 | tf_op jit(solution)/shard_map/pack/pallas_call | solution.py:370
  1.1 4.5 %chunk.2 = (f32[7,17,8,1024]{3,2,1,0:T(8,128)S(1)}, f32[16,8,1024]{2,1,0:T(8,128)S(1)}) custom-call(f32[8]{0:T(128)} %rho_tab.7, f32[8]{0:T(128)} %cond_tab.7, f32[2,32,8,1024]{3,2,1,0:T(8,128)} %bitcast.12, f32[2,2,32,8,1024]{4,3,2,1,0:T(8,128)} %bitcast.6, s32[32,8,1024]{2,1,0:T(8,128)} %bitcast.18, s32[32,8,1024]{2,1,0:T(8,128)} %bitcast.23, ...), custom_call_target="tpu_custom_call" | custom-call | flops 2000 | bytes 1500 | tf_op jit(solution)/shard_map/chunk/pallas_call | solution.py:393
  5.6 3.3 %collective-permute-start.4 = (f32[16,8,1024]{2,1,0:T(8,128)S(1)}, f32[16,8,1024]{2,1,0:T(8,128)S(1)}, u32[]{:S(2)}, u32[]{:S(2)}) collective-permute-start(f32[16,8,1024]{2,1,0:T(8,128)S(1)} %get-tuple-element.17._), channel_id=1, source_target_pairs={{64,0},{128,64},{192,128},{0,192},{65,1},{129,65},{193,129},{1,193... | collective-permute-start | bytes 1572872 | tf_op jit(solution)/shard_map/ppermute | solution.py:409
  8.9 4.7 %chunk.3 = (f32[7,17,8,1024]{3,2,1,0:T(8,128)S(1)}, f32[16,8,1024]{2,1,0:T(8,128)S(1)}, f32[16,1024]{1,0:T(8,128)S(1)}, f32[8,1024]{1,0:T(8,128)S(1)}) custom-call(f32[8]{0:T(128)} %rho_tab.7, f32[8]{0:T(128)} %cond_tab.7, f32[2,32,8,1024]{3,2,1,0:T(8,128)} %bitcast.13, f32[2,2,32,8,1024]{4,3,2,1,0:T(8,128)} %bitcast.7, s32[32,8,1024]{2,1,0:T(8,128)} %bitcast.19, ...), custom_call_target="tpu_custom_call" | custom-call | flops 2000 | bytes 1500 | tf_op jit(solution)/shard_map/chunk/pallas_call | solution.py:393
  13.6 0.1 collective-permute-start.1
  13.7 0.1 collective-permute-start
  13.8 2.2 %collective-permute-start.5 = (f32[16,1024]{1,0:T(8,128)S(1)}, f32[16,1024]{1,0:T(8,128)S(1)}, u32[]{:S(2)}, u32[]{:S(2)}) collective-permute-start(f32[16,1024]{1,0:T(8,128)S(1)} %get-tuple-element.24), channel_id=1, source_target_pairs={{0,1},{1,2},{2,3},{3,4},{4,5},{5,6},{6,7},{7,8},{8,9},{9,10},{10,1... | collective-permute-start | bytes 196616 | tf_op jit(solution)/shard_map/ppermute | solution.py:387
  16.0 1.8 %collective-permute-start.6 = (f32[8,1024]{1,0:T(8,128)S(1)}, f32[8,1024]{1,0:T(8,128)S(1)}, u32[]{:S(2)}, u32[]{:S(2)}) collective-permute-start(f32[8,1024]{1,0:T(8,128)S(1)} %get-tuple-element.25), channel_id=1, source_target_pairs={{64,1},{65,2},{66,3},{67,4},{68,5},{69,6},{70,7},{71,8},{72,9},{73... | collective-permute-start | bytes 98312 | tf_op jit(solution)/shard_map/ppermute | solution.py:388
  17.8 8.8 %collective-permute-done.6.pb = f32[8,1024]{1,0:T(8,128)S(1)} collective-permute-done((f32[8,1024]{1,0:T(8,128)S(1)}, f32[8,1024]{1,0:T(8,128)S(1)}, u32[]{:S(2)}, u32[]{:S(2)}) %collective-permute-start.6) | collective-permute-done | bytes 32800 | tf_op jit(solution)/shard_map/ppermute | solution.py:388
  26.6 1.4 %collective-permute-start.2 = (f32[16,1024]{1,0:T(8,128)S(1)}, f32[16,1024]{1,0:T(8,128)S(1)}, u32[]{:S(2)}, u32[]{:S(2)}) collective-permute-start(f32[16,1024]{1,0:T(8,128)S(1)} %get-tuple-element.22), channel_id=1, source_target_pairs={{1,0},{2,1},{3,2},{4,3},{5,4},{6,5},{7,6},{8,7},{9,8},{10,9},{11,1... | collective-permute-start | bytes 196616 | tf_op jit(solution)/shard_map/ppermute | solution.py:411
  28.1 0.0 collective-permute-done.5.pa
  28.1 8.3 %collective-permute-start.3 = (f32[8,1024]{1,0:T(8,128)S(1)}, f32[8,1024]{1,0:T(8,128)S(1)}, u32[]{:S(2)}, u32[]{:S(2)}) collective-permute-start(f32[8,1024]{1,0:T(8,128)S(1)} %get-tuple-element.23), channel_id=1, source_target_pairs={{65,0},{66,1},{67,2},{68,3},{69,4},{70,5},{71,6},{72,7},{73,8},{74... | collective-permute-start | bytes 98312 | tf_op jit(solution)/shard_map/ppermute | solution.py:412
  36.3 5.2 %second.1 = (f32[2,32,8,1024]{3,2,1,0:T(8,128)}, f32[2,8,1024]{2,1,0:T(8,128)S(1)}) custom-call(f32[7,17,8,1024]{3,2,1,0:T(8,128)S(1)} %get-tuple-element.19.w1, f32[7,17,8,1024]{3,2,1,0:T(8,128)S(1)} %get-tuple-element.20.w2, f32[2,32,8,1024]{3,2,1,0:T(8,128)} %bitcast.14, f32[2,2,32,8,1024]{4,3,2,1,0:T(8,128)} %bitcast.8), custom_call_target="tpu_custom_call" | custom-call | flops 2000 | bytes 1500 | tf_op jit(solution)/shard_map/second/pallas_call | solution.py:414
  41.5 0.0 collective-permute-done.got
  41.5 0.0 collective-permute-done.4.bulk
  41.5 2.2 %edge.2._ = f32[2,32,8,1024]{3,2,1,0:T(8,128)} custom-call(f32[8]{0:T(128)} %rho_tab.7, f32[8]{0:T(128)} %cond_tab.7, f32[2,32,8,1024]{3,2,1,0:T(8,128)} %bitcast.15, f32[2,2,32,8,1024]{4,3,2,1,0:T(8,128)} %bitcast.9, s32[32,8,1024]{2,1,0:T(8,128)} %bitcast.20, s32[32,8,1024]{2,1,0:T(8,128)} %bitcast.25, ...), custom_call_target="tpu_custom_call", output_to_operand_aliasing={{}: (11, {})} | custom-call | flops 2000 | bytes 1500 | tf_op jit(solution)/shard_map/edge/pallas_call | solution.py:426
  43.7 0.0 collective-permute-done.3.pb
  43.7 0.0 collective-permute-done.2.pa
  43.7 0.0 collective-permute-done.1.bulk
  43.7 2.2 %edge.3 = f32[2,32,8,1024]{3,2,1,0:T(8,128)} custom-call(f32[8]{0:T(128)} %rho_tab.7, f32[8]{0:T(128)} %cond_tab.7, f32[2,32,8,1024]{3,2,1,0:T(8,128)} %bitcast.16, f32[2,2,32,8,1024]{4,3,2,1,0:T(8,128)} %bitcast.10, s32[32,8,1024]{2,1,0:T(8,128)} %bitcast.21, s32[32,8,1024]{2,1,0:T(8,128)} %bitcast.26, ...), custom_call_target="tpu_custom_call", output_to_operand_aliasing={{}: (11, {})} | custom-call | flops 2000 | bytes 1500 | tf_op jit(solution)/shard_map/edge/pallas_call | solution.py:426
Async XLA Ops:
  5.6 35.9 %collective-permute-start.4 = (f32[16,8,1024]{2,1,0:T(8,128)S(1)}, f32[16,8,1024]{2,1,0:T(8,128)S(1)}, u32[]{:S(2)}, u32[]{:S(2)}) collective-permute-start(f32[16,8,1024]{2,1,0:T(8,128)S(1)} %get-tuple-element.17._), channel_id=1, source_target_pairs={{64,0},{128,64},{192,128},{0,192},{65,1},{129,65},{193,129},{1,193... | collective-permute-start | bytes 1572872 | tf_op jit(solution)/shard_map/ppermute | solution.py:409
  13.6 30.1 %collective-permute-start.1 = (f32[16,8,1024]{2,1,0:T(8,128)S(1)}, f32[16,8,1024]{2,1,0:T(8,128)S(1)}, u32[]{:S(2)}, u32[]{:S(2)}) collective-permute-start(f32[16,8,1024]{2,1,0:T(8,128)S(1)} %get-tuple-element.18), channel_id=1, source_target_pairs={{64,0},{128,64},{192,128},{0,192},{65,1},{129,65},{193,129},{1,193... | collective-permute-start | bytes 1572872 | tf_op jit(solution)/shard_map/ppermute | solution.py:410
  13.7 27.8 %collective-permute-start = (f32[6,8,1024]{2,1,0:T(8,128)S(1)}, f32[6,8,1024]{2,1,0:T(8,128)S(1)}, u32[]{:S(2)}, u32[]{:S(2)}) collective-permute-start(f32[6,8,1024]{2,1,0:T(8,128)S(1)} %get-tuple-element.16._), channel_id=1, source_target_pairs={{64,0},{128,64},{192,128},{0,192},{65,1},{129,65},{193,129},{1,193... | collective-permute-start | bytes 589832 | tf_op jit(solution)/shard_map/ppermute | solution.py:386
  13.8 14.2 %collective-permute-start.5 = (f32[16,1024]{1,0:T(8,128)S(1)}, f32[16,1024]{1,0:T(8,128)S(1)}, u32[]{:S(2)}, u32[]{:S(2)}) collective-permute-start(f32[16,1024]{1,0:T(8,128)S(1)} %get-tuple-element.24), channel_id=1, source_target_pairs={{0,1},{1,2},{2,3},{3,4},{4,5},{5,6},{6,7},{7,8},{8,9},{9,10},{10,1... | collective-permute-start | bytes 196616 | tf_op jit(solution)/shard_map/ppermute | solution.py:387
  16.0 10.6 %collective-permute-start.6 = (f32[8,1024]{1,0:T(8,128)S(1)}, f32[8,1024]{1,0:T(8,128)S(1)}, u32[]{:S(2)}, u32[]{:S(2)}) collective-permute-start(f32[8,1024]{1,0:T(8,128)S(1)} %get-tuple-element.25), channel_id=1, source_target_pairs={{64,1},{65,2},{66,3},{67,4},{68,5},{69,6},{70,7},{71,8},{72,9},{73... | collective-permute-start | bytes 98312 | tf_op jit(solution)/shard_map/ppermute | solution.py:388
  26.6 17.1 %collective-permute-start.2 = (f32[16,1024]{1,0:T(8,128)S(1)}, f32[16,1024]{1,0:T(8,128)S(1)}, u32[]{:S(2)}, u32[]{:S(2)}) collective-permute-start(f32[16,1024]{1,0:T(8,128)S(1)} %get-tuple-element.22), channel_id=1, source_target_pairs={{1,0},{2,1},{3,2},{4,3},{5,4},{6,5},{7,6},{8,7},{9,8},{10,9},{11,1... | collective-permute-start | bytes 196616 | tf_op jit(solution)/shard_map/ppermute | solution.py:411
  28.1 15.6 %collective-permute-start.3 = (f32[8,1024]{1,0:T(8,128)S(1)}, f32[8,1024]{1,0:T(8,128)S(1)}, u32[]{:S(2)}, u32[]{:S(2)}) collective-permute-start(f32[8,1024]{1,0:T(8,128)S(1)} %get-tuple-element.23), channel_id=1, source_target_pairs={{65,0},{66,1},{67,2},{68,3},{69,4},{70,5},{71,6},{72,7},{73,8},{74... | collective-permute-start | bytes 98312 | tf_op jit(solution)/shard_map/ppermute | solution.py:412

commit v2 on v0

v2 whole, which is shorter than its diff:
```python
import functools
import math

import jax
import jax.numpy as jnp
from jax import lax
from jax.experimental import pallas as pl
from jax.experimental.pallas import tpu as pltpu
from jax.sharding import PartitionSpec as P

RELAX = 0.8
KEEP_SHARE = 0.2
F32 = jnp.float32
ANY = pl.BlockSpec(memory_space=pltpu.HBM)
VMEM = pl.BlockSpec(memory_space=pltpu.VMEM)
SMEM = pl.BlockSpec(memory_space=pltpu.SMEM)
PLANES = 7
LOOK, MAKE, GO = 17, 6, 17
LANES = 128


def tables(region, *names):
    low = (region & 1) != 0
    mid = (region & 2) != 0
    top = (region & 4) != 0
    found = []
    for t in names:
        pairs = [jnp.where(low, t[2 * k + 1], t[2 * k]) for k in range(4)]
        halves = [jnp.where(mid, pairs[2 * k + 1], pairs[2 * k]) for k in range(2)]
        found.append(jnp.where(top, halves[1], halves[0]))
    return found


def row_factors(rows, radial, spacing):
    lane = lax.broadcasted_iota(jnp.int32, (rows, radial), 1)
    position = lane.astype(F32)
    cycle = 1.0 + position * spacing
    outer = 0.5 * (1.0 + (position + 0.5) * spacing)
    inner = 0.5 * (1.0 + (position - 0.5) * spacing)
    return lane, cycle, 0.5 / cycle, outer, inner


def weight_planes(rho, rho_west, rho_east, cond, dirichlet, factors):
    lane, cycle, half_cycle, outer_f, inner_f = factors
    radial = rho.shape[1]
    first, final = lane == 0, lane == radial - 1
    up = jnp.where(final, rho, pltpu.roll(rho, radial - 1, 1))
    down = jnp.where(first, rho, pltpu.roll(rho, 1, 1))
    west = (rho + rho_west) * half_cycle
    east = (rho + rho_east) * half_cycle
    outer = (rho + up) * outer_f
    inner = (rho + down) * inner_f
    mass = cond * cycle
    diagonal = mass + west + east + outer + inner
    free = dirichlet == 0
    gain = jnp.where(free, RELAX / diagonal, 0.0)
    own = jnp.where(free, KEEP_SHARE, 0.0)
    outer_gain = jnp.where(final, 0.0, gain * outer)
    inner_gain = jnp.where(first, 0.0, gain * inner)
    return own, gain * west, gain * east, outer_gain, inner_gain, gain, gain * mass


def stencil(centre, west, east, w, right):
    radial = centre.shape[1]
    up = pltpu.roll(centre, radial - 1, 1)
    down = pltpu.roll(centre, 1, 1)
    return (w[0] * centre + w[1] * west) + (w[2] * east + w[3] * up) + (w[4] * down + right)


def copy_in(src, dst, sem):
    return pltpu.make_async_copy(src, dst, sem)


def each(lo, hi, work, group):
    group = min(group, hi - lo)
    groups = -(-(hi - lo) // group)

    def step(k, _):
        at = jnp.minimum(lo + k * group, hi - group)
        work([pl.multiple_of(8 * (at + m), 8) for m in range(group)])
        return 0

    lax.fori_loop(0, groups, step, 0)


def block(v):
    return pl.ds(v * LANES, LANES)


def load_blocks(src, x, rows, sem):
    return [copy_in(src.at[:, block(v)], x.at[v, pl.ds(8, rows), :], sem.at[v]) for v in range(x.shape[0])]


def seen(x, at):
    blocks = x.shape[0]
    lane = lax.broadcasted_iota(jnp.int32, (8, LANES), 1)
    c = [x[v, pl.ds(at + 8, 8), :] for v in range(blocks)]
    left = [pltpu.roll(u, LANES - 1, 1) for u in c]
    right = [pltpu.roll(u, 1, 1) for u in c]
    out = []
    for v in range(blocks):
        up = left[v] if v == blocks - 1 else jnp.where(lane == LANES - 1, left[v + 1], left[v])
        down = right[v] if v == 0 else jnp.where(lane == 0, right[v - 1], right[v])
        out.append((c[v], x[v, pl.ds(at + 7, 8), :], x[v, pl.ds(at + 9, 8), :], up, down))
    return out


def planes_of(v, blocks, near, cond, dirichlet, factors):
    rho, rho_west, rho_east, up, down = near
    cycle, half_cycle, outer_f, inner_f = factors
    lane = lax.broadcasted_iota(jnp.int32, (8, LANES), 1)
    if v == blocks - 1:
        up = jnp.where(lane == LANES - 1, rho, up)
    if v == 0:
        down = jnp.where(lane == 0, rho, down)
    west = (rho + rho_west) * half_cycle
    east = (rho + rho_east) * half_cycle
    outer = (rho + up) * outer_f
    inner = (rho + down) * inner_f
    mass = cond * cycle
    diagonal = mass + west + east + outer + inner
    free = dirichlet == 0
    gain = jnp.where(free, RELAX / diagonal, 0.0)
    own = jnp.where(free, KEEP_SHARE, 0.0)
    outer, inner = gain * outer, gain * inner
    if v == blocks - 1:
        outer = jnp.where(lane == LANES - 1, 0.0, outer)
    if v == 0:
        inner = jnp.where(lane == 0, 0.0, inner)
    return own, gain * west, gain * east, outer, inner, gain, gain * mass


def weights_loop(reg, diri, rho_s, cond_s, fac, w_out, rho_tab, cond_tab, tiles):
    blocks = rho_s.shape[0]

    def look(ats):
        for at in ats:
            for v in range(blocks):
                r, c = tables(reg[pl.ds(at, 8), block(v)], rho_tab, cond_tab)
                rho_s[v, pl.ds(at + 8, 8), :] = r
                cond_s[pl.ds(at, 8), block(v)] = c

    each(0, tiles, look, LOOK)

    def make(ats):
        for at in ats:
            near = seen(rho_s, at)
            for v in range(blocks):
                planes = planes_of(
                    v, blocks, near[v], cond_s[pl.ds(at, 8), block(v)], diri[pl.ds(at, 8), block(v)],
                    [fac[k, :, block(v)] for k in range(4)],
                )
                for k in range(PLANES):
                    w_out[k, pl.ds(at, 8), block(v)] = planes[k]

    each(0, tiles, make, MAKE)


def sweep(x, y, w, w_at, src, right, first, lo, hi, plain_at=None):
    blocks = x.shape[0]

    def go(ats):
        for at in ats:
            near = seen(x, at)
            wt = pl.multiple_of(at - 8 * w_at, 8)
            for v in range(blocks):
                c, west, east, up, down = near[v]
                p = [w[k, pl.ds(wt, 8), block(v)] for k in range(PLANES if first else 5)]
                if first:
                    b = p[5] * src[pl.ds(at, 8), block(v)] + p[6] * c
                    right[pl.ds(at, 8), block(v)] = b
                else:
                    b = right[pl.ds(at, 8), block(v)]
                new = (p[0] * c + p[1] * west) + (p[2] * east + p[3] * up) + (p[4] * down + b)
                if plain_at is None:
                    y[v, pl.ds(at + 8, 8), :] = new
                else:
                    y[pl.ds(pl.multiple_of(at - 8 * plain_at, 8), 8), block(v)] = new

    each(lo, hi, go, GO)


def own_kernel(rows, rho_tab, cond_tab, end, source, region, diri, own, reg1, dir1, splat, rt, ct, sems):
    last = end.shape[1] - 8
    copies = [copy_in(rho_tab, rt, sems.at[0]), copy_in(cond_tab, ct, sems.at[1])]
    for side, at in ((0, 0), (1, last)):
        for k, src in enumerate((end.at[0], source.at[0, 0], source.at[0, 1])):
            copies.append(copy_in(src.at[pl.ds(at, 8), :], own.at[3 * side + k], sems.at[2 + 3 * side + k]))
    copies.append(copy_in(region.at[pl.ds(0, rows), :], reg1, sems.at[8]))
    copies.append(copy_in(diri.at[pl.ds(0, rows), :], dir1, sems.at[9]))
    for c in copies:
        c.start()
    for c in copies[:2]:
        c.wait()
    for k in range(8):
        splat[k] = jnp.full((8, LANES), rt[k], F32)
        splat[8 + k] = jnp.full((8, LANES), ct[k], F32)
    for c in copies[2:]:
        c.wait()


def edge_loads(end, source, region, diri, side, buf, regs, sems):
    rows = pl.ds(side * (end.shape[1] - 8), 8)
    return [
        copy_in(end.at[1, rows, :], buf.at[0], sems.at[0]),
        copy_in(source.at[1, 0, rows, :], buf.at[1], sems.at[1]),
        copy_in(source.at[1, 1, rows, :], buf.at[2], sems.at[2]),
        copy_in(region.at[rows, :], regs.at[0], sems.at[3]),
        copy_in(diri.at[rows, :], regs.at[1], sems.at[4]),
    ]


def write_pack(buf, regs, got, out, side):
    pick = (lambda m: slice(0, m)) if side == 0 else (lambda m: slice(8 - m, 8))
    for at, parts in ((0, [buf[k] for k in range(3)]), (8, [got[3 * side + k] for k in range(3)])):
        out[at : at + 4, :] = parts[0][pick(4), :]
        out[at + 4 : at + 7, :] = parts[1][pick(3), :]
        out[at + 7 : at + 8, :] = parts[2][pick(1), :]
    out[16:20, :] = regs[0, pick(4), :].astype(F32)
    out[20:23, :] = regs[1, pick(3), :].astype(F32)
    out[23:24, :] = jnp.zeros((1, out.shape[1]), F32)


def pack_kernel(buf, regs, got, up):
    write_pack(buf, regs, got, up, 1)


def chunk_kernel(base, tiles, lo, hi, spacing, first, splat, reg_v, dir_v, end, source, region, diri, got, *refs):
    refs = refs if first else refs[1:]
    w_out, chunk, buf, regs = refs[:4]
    x, y, s0, s1, right, rho_s, cond_s, fac, sems, x_sems, edge_sems = refs[-11:]
    n, radial = end.shape[1:]
    rows = pl.ds(8 * base, 8 * tiles)
    state = load_blocks(end.at[0, rows], x, 8 * tiles, x_sems.at[0])
    later = [copy_in(source.at[0, 0, rows, :], s0, sems.at[0]), copy_in(source.at[0, 1, rows, :], s1, sems.at[1])]
    ahead = edge_loads(end, source, region, diri, 1 if first else 0, buf, regs, edge_sems)
    if first:
        reg2, dir2 = refs[4:6]
        ends = pl.ds(n - 8 * tiles, 8 * tiles)
        ahead += [copy_in(region.at[ends, :], reg2, sems.at[2]), copy_in(diri.at[ends, :], dir2, sems.at[3])]
    else:
        dn, x1, s10, s11 = refs[4:8]
        ahead += load_blocks(end.at[1], x1, n, x_sems.at[1])
        ahead += [copy_in(source.at[1, 0], s10, sems.at[2]), copy_in(source.at[1, 1], s11, sems.at[3])]
    for c in state + later + ahead:
        c.start()
    _, cycle, half, outer, inner = row_factors(8, radial, spacing)
    for k, f in enumerate((cycle, half, outer, inner)):
        fac[k] = f
    weights_loop(
        reg_v, dir_v, rho_s, cond_s, fac, w_out,
        [splat[k] for k in range(8)], [splat[8 + k] for k in range(8)], tiles,
    )
    for c in state + later[:1]:
        c.wait()
    sweep(x, y, w_out, 0, s0, right, True, 0, tiles)
    sweep(y, x, w_out, 0, None, right, False, 0, tiles)
    later[1].wait()
    sweep(x, y, w_out, 0, s1, right, True, 0, tiles)
    sweep(y, chunk, w_out, 0, None, right, False, lo, hi, lo)
    for c in ahead:
        c.wait()
    if not first:
        write_pack(buf, regs, got, dn, 0)


def second_kernel(w1, w2, x1, s0, s1, out, ends, x, y, right, plain, sems):
    rows = s0.shape[0]
    tiles = rows // 8
    half = tiles // 2
    skip = tiles - w2.shape[1] // 8

    def both(a, b, src, first, plain_at=None, after=None):
        for k, w, at in ((0, w1, 0), (1, w2, skip)):
            sweep(a, b, w, at, src, right, first, k * half, (k + 1) * half, plain_at)
            if after:
                after(k)

    def back(k):
        piece = pl.ds(8 * k * half, 8 * half)
        return copy_in(plain.at[piece, :], out.at[0, piece, :], sems.at[k])

    both(x1, y, s0, True)
    both(y, x, None, False)
    both(x, y, s1, True)
    both(y, plain, None, False, 0, lambda k: back(k).start())
    ends[0] = plain[0:8, :]
    ends[1] = plain[rows - 8 : rows, :]
    for k in range(2):
        back(k).wait()


def edge_kernel(
    side, spacing,
    splat, own, regs, got, bulk, ends, pack, _,
    out,
    xw, sw, rw, dw, tiles_out, sems,
):
    half, radial = bulk.shape
    rows = 2 * half
    at = pl.ds(side * (rows - 8), 8)
    moved = copy_in(
        bulk.at[pl.ds(8 - 8 * side, half - 8), :], out.at[1, pl.ds(half if side else 8, half - 8), :], sems.at[0]
    )
    moved.start()
    factors = row_factors(16, radial, spacing)
    zero = jnp.zeros((16, radial), F32)
    mine = 8 if side == 0 else 0
    halo = (lambda m: slice(8 - m, 8)) if side == 0 else (lambda m: slice(8, 8 + m))
    rw[...] = jnp.zeros((16, radial), jnp.int32)
    dw[...] = jnp.zeros((16, radial), jnp.int32)
    rw[halo(4), :] = pack[16:20, :].astype(jnp.int32)
    dw[halo(3), :] = pack[20:23, :].astype(jnp.int32)
    for p in range(2):
        xw[p] = zero
        sw[p, 0] = zero
        sw[p, 1] = zero
        xw[p, halo(4), :] = pack[8 * p : 8 * p + 4, :]
        sw[p, 0, halo(3), :] = pack[8 * p + 4 : 8 * p + 7, :]
        sw[p, 1, halo(1), :] = pack[8 * p + 7 : 8 * p + 8, :]
    xw[1, mine : mine + 8, :] = got[3 * side]
    sw[1, 0, mine : mine + 8, :] = got[3 * side + 1]
    sw[1, 1, mine : mine + 8, :] = got[3 * side + 2]
    rw[mine : mine + 8, :] = regs[0]
    dw[mine : mine + 8, :] = regs[1]
    xw[0, mine : mine + 8, :] = own[0]
    sw[0, 0, mine : mine + 8, :] = own[1]
    sw[0, 1, mine : mine + 8, :] = own[2]
    found = [
        tables(rw[:, block(v)], *[[jnp.concatenate([splat[8 * q + k]] * 2) for k in range(8)] for q in range(2)])
        for v in range(radial // LANES)
    ]
    rho = jnp.concatenate([u[0] for u in found], axis=1)
    cond = jnp.concatenate([u[1] for u in found], axis=1)
    w = weight_planes(rho, pltpu.roll(rho, 1, 0), pltpu.roll(rho, 15, 0), cond, dw[...], factors)
    state = [xw[0], xw[1]]
    for step in range(2):
        right = [w[5] * sw[p, step] + w[6] * state[p] for p in range(2)]
        for _ in range(2):
            state = [
                stencil(v, pltpu.roll(v, 1, 0), pltpu.roll(v, 15, 0), w, r) for v, r in zip(state, right)
            ]
    sub = lax.broadcasted_iota(jnp.int32, (8, radial), 0)
    edge = sub < 4 if side == 0 else sub >= 4
    stores = []
    for p, keep in ((0, ends[side]), (1, bulk[side * (half - 8) : side * (half - 8) + 8, :])):
        tiles_out[p] = jnp.where(edge, state[p][mine : mine + 8, :], keep)
        stores.append(copy_in(tiles_out.at[p], out.at[p, at, :], sems.at[1 + p]))
        stores[-1].start()
    for c in [moved] + stores:
        c.wait()


def params(mib):
    return pltpu.CompilerParams(vmem_limit_bytes=mib * 2**20)


def cost(us):
    return pl.CostEstimate(flops=int(us * 4e3), bytes_accessed=int(us * 3e3), transcendentals=0)


def body(end, source, region, diri, rho_tab, cond_tab):
    n, radial = end.shape[1], end.shape[2]
    devices, rings = lax.axis_size("space"), lax.axis_size("tm")
    spacing = 2.0 * math.pi / (n * devices)
    tiles = n // 8
    part = tiles // 2 + 1
    blocks = radial // LANES
    dma = pltpu.SemaphoreType.DMA

    def f(*shape):
        return jax.ShapeDtypeStruct(shape + (radial,), F32)

    def buf(*shape):
        return pltpu.VMEM(shape + (radial,), F32)

    def ints(*shape):
        return pltpu.VMEM(shape + (radial,), jnp.int32)

    def cut(rows):
        return pltpu.VMEM((blocks, rows + 16, LANES), F32)

    held = [pltpu.with_memory_space_constraint(v, pltpu.HBM) for v in (end, source, region, diri)]
    tabs = [pltpu.with_memory_space_constraint(v, pltpu.HBM) for v in (rho_tab, cond_tab)]
    tab_s = [pltpu.SMEM((rho_tab.shape[0],), F32)] * 2
    edge_o = [buf(3, 8), ints(2, 8)]

    up = [(s, (s + 1) % devices) for s in range(devices)]
    down = [(b, a) for a, b in up]
    back = [((t + 1) % rings, t) for t in range(rings)]

    rows = 8 * part
    own, reg1, dir1, splat = pl.pallas_call(
        functools.partial(own_kernel, rows),
        name="own",
        out_shape=[f(6, 8), ints(rows), ints(rows), pltpu.VMEM((16, 8, LANES), F32)],
        in_specs=[ANY] * 6,
        out_specs=[VMEM] * 4,
        scratch_shapes=tab_s + [dma((10,))],
        compiler_params=params(16),
        cost_estimate=cost(1),
    )(*tabs, *held)
    got = lax.ppermute(own, "tm", back)

    def chunk(base, lo, hi, reg, dirs, got, extra):
        return pl.pallas_call(
            functools.partial(chunk_kernel, base, part, lo, hi, spacing, base == 0),
            name="chunk",
            out_shape=[pltpu.VMEM((PLANES, rows, radial), F32), f(8 * (hi - lo))] + edge_o + extra,
            in_specs=[VMEM] * 3 + [ANY] * 4 + [VMEM] * len(got),
            out_specs=[VMEM] * (4 + len(extra)),
            scratch_shapes=[cut(rows), cut(rows), buf(rows), buf(rows), buf(rows), cut(rows), buf(rows), buf(4, 8)]
            + [dma((4,)), dma((2, blocks)), dma((5,))],
            compiler_params=params(20),
            cost_estimate=cost(1),
        )(splat, reg, dirs, *held, *got)

    w1, c1, buf1, regs1, reg2, dir2 = chunk(0, 0, part - 1, reg1, dir1, [own], [ints(rows), ints(rows)])
    pack = pl.pallas_call(
        pack_kernel,
        name="pack",
        out_shape=f(24),
        in_specs=[VMEM] * 3,
        out_specs=VMEM,
        compiler_params=params(16),
        cost_estimate=cost(1),
    )(buf1, regs1, got)
    w2, c2, buf0, regs0, dn, x1, s10, s11 = chunk(
        tiles - part, 1, part, reg2, dir2, [got, pack], [f(24), cut(n), buf(n), buf(n)]
    )
    c1 = lax.ppermute(c1, "tm", back)
    c2 = lax.ppermute(c2, "tm", back)
    pack = lax.ppermute(pack, "space", up)
    dn = lax.ppermute(dn, "space", down)

    out, ends = pl.pallas_call(
        second_kernel,
        name="second",
        out_shape=[f(2, n), f(2, 8)],
        in_specs=[VMEM] * 5,
        out_specs=[ANY, VMEM],
        scratch_shapes=[cut(n), cut(n), buf(n), buf(n), dma((2,))],
        compiler_params=params(20),
        cost_estimate=cost(1),
    )(w1, w2, x1, s10, s11)

    for side, bulk, halo, edge in ((0, c1, pack, (buf0, regs0)), (1, c2, dn, (buf1, regs1))):
        out = pl.pallas_call(
            functools.partial(edge_kernel, side, spacing),
            name="edge",
            out_shape=f(2, n),
            in_specs=[VMEM] * 7 + [ANY],
            out_specs=ANY,
            scratch_shapes=[buf(2, 16), buf(2, 2, 16), ints(16), ints(16), buf(2, 8), dma((3,))],
            input_output_aliases={7: 0},
            compiler_params=params(20),
            cost_estimate=cost(100 if side == 0 else 1),
        )(splat, *edge, got, bulk, ends, halo, out)
    return out


def solution(mesh):
    return jax.shard_map(
        body,
        mesh=mesh,
        in_specs=(
            P("tm", "space", None),
            P("tm", None, "space", None),
            P("space", None),
            P("space", None),
            P(),
            P(),
        ),
        out_specs=P("tm", "space", None),
        check_vma=False,
    )
```

time: 98.6 us -> 28.3 us (0.29)
  the two profiles are of different devices: /device:TPU:1 before, /device:TPU:6 now
where the time goes in v2:
time: 28.3 us; the launch traced here: 28.1 us
  Pallas kernels  13.5 us (48%)
  waiting for transfers between devices  8.74 us (31%)
  starting transfers between devices  5.78 us (20%)
    ppermute x1, waiting for transfers between devices, body(): pack = lax.ppermute(pack, 'space', up)  8.73 us
    pallas_call x2, Pallas kernels, chunk(): pl.pallas_call(functools.partial(chunk_kernel, base, part, lo, hi, spacin...  6.41 us
    pallas_call x1, Pallas kernels, body(): pl.pallas_call(second_kernel, name='second', out_shape=[f(2, n), f(2, 8)]...  3.22 us
    pallas_call x2, Pallas kernels, body(): pl.pallas_call(functools.partial(edge_kernel, side, spacing), name='edge'...  2.47 us
    ppermute x1, starting transfers between devices, body(): pack = lax.ppermute(pack, 'space', up)  2.16 us
    pallas_call x1, Pallas kernels, body(): pl.pallas_call(functools.partial(own_kernel, rows), name='own', out_shape...  1.43 us
    ppermute x1, starting transfers between devices, body(): dn = lax.ppermute(dn, 'space', down)  1.37 us
    ppermute x1, starting transfers between devices, body(): c2 = lax.ppermute(c2, 'tm', back)  1.15 us
  transfers between devices with their start and end apart: 5, of which 1 were waited for; matrix products, arithmetic and copies ran while one was open for 0% of the time, Pallas kernels for 39%

profile of v2, /device:TPU:6, one launch (start us, length us, event | category | flops | bytes accessed | tf_op | source)
XLA Modules:
  0.0 28.1 jit_solution(2457899139568757831)
XLA Ops:
  0.0 1.4 %own.1 = (f32[6,8,1024]{2,1,0:T(8,128)S(1)}, s32[136,1024]{1,0:T(8,128)S(1)}, s32[136,1024]{1,0:T(8,128)S(1)}, f32[16,8,128]{2,1,0:T(8,128)S(1)}) custom-call(f32[8]{0:T(128)} %rho_tab.1, f32[8]{0:T(128)} %cond_tab.1, f32[2,256,1024]{2,1,0:T(8,128)} %end.5, f32[2,2,256,1024]{3,2,1,0:T(8,128)} %source.5, s32[256,1024]{1,0:T(8,128)} %region.5, s32[256,1024]{1,0:T(8,128)} %diri.5), custom_call_target="tpu_custom_call" | custom-call | flops 4000 | bytes 3000 | tf_op jit(solution)/shard_map/own/pallas_call | solution.py:393
  1.4 0.3 %collective-permute-start = (f32[6,8,1024]{2,1,0:T(8,128)S(1)}, f32[6,8,1024]{2,1,0:T(8,128)S(1)}, u32[]{:S(2)}, u32[]{:S(2)}) collective-permute-start(f32[6,8,1024]{2,1,0:T(8,128)S(1)} %get-tuple-element.28.got), channel_id=1, source_target_pairs={{64,0},{128,64},{192,128},{0,192},{65,1},{129,65},{193,129},{1,193... | collective-permute-start | bytes 589832 | tf_op jit(solution)/shard_map/ppermute | solution.py:403
  1.8 3.3 %chunk.2 = (f32[7,136,1024]{2,1,0:T(8,128)S(1)}, f32[128,1024]{1,0:T(8,128)S(1)}, f32[3,8,1024]{2,1,0:T(8,128)S(1)}, s32[2,8,1024]{2,1,0:T(8,128)S(1)}, s32[136,...) custom-call(f32[16,8,128]{2,1,0:T(8,128)S(1)} %get-tuple-element.25.splat, s32[136,1024]{1,0:T(8,128)S(1)} %get-tuple-element.26.reg_v, ...), custom_call_target="tpu_custom_call" | custom-call | flops 4000 | bytes 3000 | tf_op jit(solution)/shard_map/chunk/pallas_call | solution.py:406
  5.0 0.8 %collective-permute-start.3 = (f32[128,1024]{1,0:T(8,128)S(1)}, f32[128,1024]{1,0:T(8,128)S(1)}, u32[]{:S(2)}, u32[]{:S(2)}) collective-permute-start(f32[128,1024]{1,0:T(8,128)S(1)} %get-tuple-element.43), channel_id=1, source_target_pairs={{64,0},{128,64},{192,128},{0,192},{65,1},{129,65},{193,129},{1,193... | collective-permute-start | bytes 1572872 | tf_op jit(solution)/shard_map/ppermute | solution.py:431
  5.8 0.0 collective-permute-done.got
  5.8 3.2 %chunk.3 = (f32[7,136,1024]{2,1,0:T(8,128)S(1)}, f32[128,1024]{1,0:T(8,128)S(1)}, f32[3,8,1024]{2,1,0:T(8,128)S(1)}, s32[2,8,1024]{2,1,0:T(8,128)S(1)}, f32[24,1...) custom-call(f32[16,8,128]{2,1,0:T(8,128)S(1)} %get-tuple-element.25.splat, ...), custom_call_target="tpu_custom_call" | custom-call | flops 4000 | bytes 3000 | tf_op jit(solution)/shard_map/chunk/pallas_call | solution.py:406
  9.0 1.2 %collective-permute-start.1 = (f32[128,1024]{1,0:T(8,128)S(1)}, f32[128,1024]{1,0:T(8,128)S(1)}, u32[]{:S(2)}, u32[]{:S(2)}) collective-permute-start(f32[128,1024]{1,0:T(8,128)S(1)} %get-tuple-element.33), channel_id=1, source_target_pairs={{64,0},{128,64},{192,128},{0,192},{65,1},{129,65},{193,129},{1,193... | collective-permute-start | bytes 1572872 | tf_op jit(solution)/shard_map/ppermute | solution.py:432
  10.1 2.2 %collective-permute-start.4 = (f32[24,1024]{1,0:T(8,128)S(1)}, f32[24,1024]{1,0:T(8,128)S(1)}, u32[]{:S(2)}, u32[]{:S(2)}) collective-permute-start(f32[24,1024]{1,0:T(8,128)S(1)} %pack.1.refs_0_), channel_id=1, source_target_pairs={{0,1},{1,2},{2,3},{3,4},{4,5},{5,6},{6,7},{7,8},{8,9},{9,10},{10,1... | collective-permute-start | bytes 294920 | tf_op jit(solution)/shard_map/ppermute | solution.py:433
  12.3 1.4 %collective-permute-start.2 = (f32[24,1024]{1,0:T(8,128)S(1)}, f32[24,1024]{1,0:T(8,128)S(1)}, u32[]{:S(2)}, u32[]{:S(2)}) collective-permute-start(f32[24,1024]{1,0:T(8,128)S(1)} %get-tuple-element.40), channel_id=1, source_target_pairs={{1,0},{2,1},{3,2},{4,3},{5,4},{6,5},{7,6},{8,7},{9,8},{10,9},{11,1... | collective-permute-start | bytes 294920 | tf_op jit(solution)/shard_map/ppermute | solution.py:434
  13.7 3.2 %second.1 = (f32[2,256,1024]{2,1,0:T(8,128)}, f32[2,8,1024]{2,1,0:T(8,128)S(1)}) custom-call(f32[7,136,1024]{2,1,0:T(8,128)S(1)} %get-tuple-element.34.w1, f32[7,136,1024]{2,1,0:T(8,128)S(1)} %get-tuple-element.35.w2, f32[8,272,128]{2,1,0:T(8,128)S(1)} %get-tuple-element.36.x1, f32[256,1024]{1,0:T(8,128)S(1)} %get-tuple-element.37.s0, ...), custom_call_target="tpu_custom_call" | custom-call | flops 4000 | bytes 3000 | tf_op jit(solution)/shard_map/second/pallas_call | solution.py:436
  16.9 8.7 %collective-permute-done.4.pack = f32[24,1024]{1,0:T(8,128)S(1)} collective-permute-done((f32[24,1024]{1,0:T(8,128)S(1)}, f32[24,1024]{1,0:T(8,128)S(1)}, u32[]{:S(2)}, u32[]{:S(2)}) %collective-permute-start.4) | collective-permute-done | bytes 98336 | tf_op jit(solution)/shard_map/ppermute | solution.py:433
  25.6 0.0 collective-permute-done.3.bulk
  25.6 1.3 %edge.2._ = f32[2,256,1024]{2,1,0:T(8,128)} custom-call(f32[16,8,128]{2,1,0:T(8,128)S(1)} %get-tuple-element.25.splat, f32[3,8,1024]{2,1,0:T(8,128)S(1)} %get-tuple-element.41.own, s32[2,8,1024]{2,1,0:T(8,128)S(1)} %get-tuple-element.42.regs, f32[6,8,1024]{2,1,0:T(8,128)S(1)} %collective-permute-done.got, ...), custom_call_target="tpu_custom_call", output_to_operand_aliasing={{}: (7, {})} | custom-call | flops 400000 | bytes 300000 | tf_op jit(solution)/shard_map/edge/pallas_call | solution.py:448
  26.9 0.0 collective-permute-done.2.pack
  26.9 0.0 collective-permute-done.1.bulk
  27.0 1.2 %edge.3 = f32[2,256,1024]{2,1,0:T(8,128)} custom-call(f32[16,8,128]{2,1,0:T(8,128)S(1)} %get-tuple-element.25.splat, f32[3,8,1024]{2,1,0:T(8,128)S(1)} %get-tuple-element.29.buf.own, s32[2,8,1024]{2,1,0:T(8,128)S(1)} %get-tuple-element.30.regs, f32[6,8,1024]{2,1,0:T(8,128)S(1)} %collective-permute-done.got, ...), custom_call_target="tpu_custom_call", output_to_operand_aliasing={{}: (7, {})} | custom-call | flops 4000 | bytes 3000 | tf_op jit(solution)/shard_map/edge/pallas_call | solution.py:448
  (1 shorter events, 0.0 us)
Async XLA Ops:
  1.4 4.4 %collective-permute-start = (f32[6,8,1024]{2,1,0:T(8,128)S(1)}, f32[6,8,1024]{2,1,0:T(8,128)S(1)}, u32[]{:S(2)}, u32[]{:S(2)}) collective-permute-start(f32[6,8,1024]{2,1,0:T(8,128)S(1)} %get-tuple-element.28.got), channel_id=1, source_target_pairs={{64,0},{128,64},{192,128},{0,192},{65,1},{129,65},{193,129},{1,193... | collective-permute-start | bytes 589832 | tf_op jit(solution)/shard_map/ppermute | solution.py:403
  5.0 20.6 %collective-permute-start.3 = (f32[128,1024]{1,0:T(8,128)S(1)}, f32[128,1024]{1,0:T(8,128)S(1)}, u32[]{:S(2)}, u32[]{:S(2)}) collective-permute-start(f32[128,1024]{1,0:T(8,128)S(1)} %get-tuple-element.43), channel_id=1, source_target_pairs={{64,0},{128,64},{192,128},{0,192},{65,1},{129,65},{193,129},{1,193... | collective-permute-start | bytes 1572872 | tf_op jit(solution)/shard_map/ppermute | solution.py:431
  9.0 18.0 %collective-permute-start.1 = (f32[128,1024]{1,0:T(8,128)S(1)}, f32[128,1024]{1,0:T(8,128)S(1)}, u32[]{:S(2)}, u32[]{:S(2)}) collective-permute-start(f32[128,1024]{1,0:T(8,128)S(1)} %get-tuple-element.33), channel_id=1, source_target_pairs={{64,0},{128,64},{192,128},{0,192},{65,1},{129,65},{193,129},{1,193... | collective-permute-start | bytes 1572872 | tf_op jit(solution)/shard_map/ppermute | solution.py:432
  10.1 15.5 %collective-permute-start.4 = (f32[24,1024]{1,0:T(8,128)S(1)}, f32[24,1024]{1,0:T(8,128)S(1)}, u32[]{:S(2)}, u32[]{:S(2)}) collective-permute-start(f32[24,1024]{1,0:T(8,128)S(1)} %pack.1.refs_0_), channel_id=1, source_target_pairs={{0,1},{1,2},{2,3},{3,4},{4,5},{5,6},{6,7},{7,8},{8,9},{9,10},{10,1... | collective-permute-start | bytes 294920 | tf_op jit(solution)/shard_map/ppermute | solution.py:433
  12.3 14.6 %collective-permute-start.2 = (f32[24,1024]{1,0:T(8,128)S(1)}, f32[24,1024]{1,0:T(8,128)S(1)}, u32[]{:S(2)}, u32[]{:S(2)}) collective-permute-start(f32[24,1024]{1,0:T(8,128)S(1)} %get-tuple-element.40), channel_id=1, source_target_pairs={{1,0},{2,1},{3,2},{4,3},{5,4},{6,5},{7,6},{8,7},{9,8},{10,9},{11,1... | collective-permute-start | bytes 294920 | tf_op jit(solution)/shard_map/ppermute | solution.py:434

commit v3 on v2

--- a/solution.py
+++ b/solution.py
@@ -15,7 +15,7 @@
 VMEM = pl.BlockSpec(memory_space=pltpu.VMEM)
 SMEM = pl.BlockSpec(memory_space=pltpu.SMEM)
 PLANES = 7
-LOOK, MAKE, GO = 17, 6, 17
+LOOK, MAKE, GO = 9, 6, 17
 LANES = 128
 
 
@@ -291,63 +291,77 @@
 
 
 def edge_kernel(
-    side, spacing,
-    splat, own, regs, got, bulk, ends, pack, _,
-    out,
-    xw, sw, rw, dw, tiles_out, sems,
+    spacing, splat, own0, regs0, own1, regs1, got, ends, from_up, from_down, *refs
 ):
-    half, radial = bulk.shape
-    rows = 2 * half
-    at = pl.ds(side * (rows - 8), 8)
-    moved = copy_in(
-        bulk.at[pl.ds(8 - 8 * side, half - 8), :], out.at[1, pl.ds(half if side else 8, half - 8), :], sems.at[0]
-    )
-    moved.start()
+    *bulk, _, out, xw, sw, rw, dw, tiles_out, sems = refs
+    rows, radial = out.shape[1:]
+    moved = []
+    row = 0
+    for k, b in enumerate(bulk):
+        skip = 8 if k == 0 else 0
+        size = b.shape[0] - skip - (8 if k + 1 == len(bulk) else 0)
+        moved.append(copy_in(b.at[pl.ds(skip, size), :], out.at[1, pl.ds(row + skip, size), :], sems.at[4 + k]))
+        row += b.shape[0]
+    for c in moved:
+        c.start()
     factors = row_factors(16, radial, spacing)
     zero = jnp.zeros((16, radial), F32)
-    mine = 8 if side == 0 else 0
-    halo = (lambda m: slice(8 - m, 8)) if side == 0 else (lambda m: slice(8, 8 + m))
-    rw[...] = jnp.zeros((16, radial), jnp.int32)
-    dw[...] = jnp.zeros((16, radial), jnp.int32)
-    rw[halo(4), :] = pack[16:20, :].astype(jnp.int32)
-    dw[halo(3), :] = pack[20:23, :].astype(jnp.int32)
-    for p in range(2):
-        xw[p] = zero
-        sw[p, 0] = zero
-        sw[p, 1] = zero
-        xw[p, halo(4), :] = pack[8 * p : 8 * p + 4, :]
-        sw[p, 0, halo(3), :] = pack[8 * p + 4 : 8 * p + 7, :]
-        sw[p, 1, halo(1), :] = pack[8 * p + 7 : 8 * p + 8, :]
-    xw[1, mine : mine + 8, :] = got[3 * side]
-    sw[1, 0, mine : mine + 8, :] = got[3 * side + 1]
-    sw[1, 1, mine : mine + 8, :] = got[3 * side + 2]
-    rw[mine : mine + 8, :] = regs[0]
-    dw[mine : mine + 8, :] = regs[1]
-    xw[0, mine : mine + 8, :] = own[0]
-    sw[0, 0, mine : mine + 8, :] = own[1]
-    sw[0, 1, mine : mine + 8, :] = own[2]
-    found = [
-        tables(rw[:, block(v)], *[[jnp.concatenate([splat[8 * q + k]] * 2) for k in range(8)] for q in range(2)])
-        for v in range(radial // LANES)
-    ]
-    rho = jnp.concatenate([u[0] for u in found], axis=1)
-    cond = jnp.concatenate([u[1] for u in found], axis=1)
-    w = weight_planes(rho, pltpu.roll(rho, 1, 0), pltpu.roll(rho, 15, 0), cond, dw[...], factors)
-    state = [xw[0], xw[1]]
+    weights, state = [], []
+    for side, own, regs, pack in ((0, own0, regs0, from_up), (1, own1, regs1, from_down)):
+        mine = 8 if side == 0 else 0
+        halo = (lambda m: slice(8 - m, 8)) if side == 0 else (lambda m: slice(8, 8 + m))
+        rw[side] = jnp.zeros((16, radial), jnp.int32)
+        dw[side] = jnp.zeros((16, radial), jnp.int32)
+        rw[side, halo(4), :] = pack[16:20, :].astype(jnp.int32)
+        dw[side, halo(3), :] = pack[20:23, :].astype(jnp.int32)
+        rw[side, mine : mine + 8, :] = regs[0]
+        dw[side, mine : mine + 8, :] = regs[1]
+        for p in range(2):
+            xw[side, p] = zero
+            sw[side, p, 0] = zero
+            sw[side, p, 1] = zero
+            xw[side, p, halo(4), :] = pack[8 * p : 8 * p + 4, :]
+            sw[side, p, 0, halo(3), :] = pack[8 * p + 4 : 8 * p + 7, :]
+            sw[side, p, 1, halo(1), :] = pack[8 * p + 7 : 8 * p + 8, :]
+            parts = [own[k] for k in range(3)] if p == 0 else [got[3 * side + k] for k in range(3)]
+            xw[side, p, mine : mine + 8, :] = parts[0]
+            sw[side, p, 0, mine : mine + 8, :] = parts[1]
+            sw[side, p, 1, mine : mine + 8, :] = parts[2]
+        found = [
+            tables(
+                rw[side, :, block(v)],
+                *[[jnp.concatenate([splat[8 * q + k]] * 2) for k in range(8)] for q in range(2)],
+            )
+            for v in range(radial // LANES)
+        ]
+        rho = jnp.concatenate([u[0] for u in found], axis=1)
+        cond = jnp.concatenate([u[1] for u in found], axis=1)
+        weights.append(
+            weight_planes(rho, pltpu.roll(rho, 1, 0), pltpu.roll(rho, 15, 0), cond, dw[side], factors)
+        )
+        state += [(side, p, xw[side, p]) for p in range(2)]
     for step in range(2):
-        right = [w[5] * sw[p, step] + w[6] * state[p] for p in range(2)]
+        right = [weights[side][5] * sw[side, p, step] + weights[side][6] * v for side, p, v in state]
         for _ in range(2):
             state = [
-                stencil(v, pltpu.roll(v, 1, 0), pltpu.roll(v, 15, 0), w, r) for v, r in zip(state, right)
+                (side, p, stencil(v, pltpu.roll(v, 1, 0), pltpu.roll(v, 15, 0), weights[side], r))
+                for (side, p, v), r in zip(state, right)
             ]
     sub = lax.broadcasted_iota(jnp.int32, (8, radial), 0)
-    edge = sub < 4 if side == 0 else sub >= 4
     stores = []
-    for p, keep in ((0, ends[side]), (1, bulk[side * (half - 8) : side * (half - 8) + 8, :])):
-        tiles_out[p] = jnp.where(edge, state[p][mine : mine + 8, :], keep)
-        stores.append(copy_in(tiles_out.at[p], out.at[p, at, :], sems.at[1 + p]))
+    for k, (side, p, v) in enumerate(state):
+        mine = 8 if side == 0 else 0
+        if p == 0:
+            keep = ends[side]
+        else:
+            keep = bulk[0][0:8, :] if side == 0 else bulk[-1][bulk[-1].shape[0] - 8 :, :]
+        edge = sub < 4 if side == 0 else sub >= 4
+        tiles_out[k] = jnp.where(edge, v[mine : mine + 8, :], keep)
+        stores.append(
+            copy_in(tiles_out.at[k], out.at[p, pl.ds(side * (rows - 8), 8), :], sems.at[k])
+        )
         stores[-1].start()
-    for c in [moved] + stores:
+    for c in moved + stores:
         c.wait()
 
 
@@ -397,7 +411,7 @@
         in_specs=[ANY] * 6,
         out_specs=[VMEM] * 4,
         scratch_shapes=tab_s + [dma((10,))],
-        compiler_params=params(16),
+        compiler_params=params(10),
         cost_estimate=cost(1),
     )(*tabs, *held)
     got = lax.ppermute(own, "tm", back)
@@ -411,7 +425,7 @@
             out_specs=[VMEM] * (4 + len(extra)),
             scratch_shapes=[cut(rows), cut(rows), buf(rows), buf(rows), buf(rows), cut(rows), buf(rows), buf(4, 8)]
             + [dma((4,)), dma((2, blocks)), dma((5,))],
-            compiler_params=params(20),
+            compiler_params=params(10),
             cost_estimate=cost(1),
         )(splat, reg, dirs, *held, *got)
 
@@ -422,7 +436,7 @@
         out_shape=f(24),
         in_specs=[VMEM] * 3,
         out_specs=VMEM,
-        compiler_params=params(16),
+        compiler_params=params(10),
         cost_estimate=cost(1),
     )(buf1, regs1, got)
     w2, c2, buf0, regs0, dn, x1, s10, s11 = chunk(
@@ -440,23 +454,22 @@
         in_specs=[VMEM] * 5,
         out_specs=[ANY, VMEM],
         scratch_shapes=[cut(n), cut(n), buf(n), buf(n), dma((2,))],
-        compiler_params=params(20),
+        compiler_params=params(10),
         cost_estimate=cost(1),
     )(w1, w2, x1, s10, s11)
 
-    for side, bulk, halo, edge in ((0, c1, pack, (buf0, regs0)), (1, c2, dn, (buf1, regs1))):
-        out = pl.pallas_call(
-            functools.partial(edge_kernel, side, spacing),
-            name="edge",
-            out_shape=f(2, n),
-            in_specs=[VMEM] * 7 + [ANY],
-            out_specs=ANY,
-            scratch_shapes=[buf(2, 16), buf(2, 2, 16), ints(16), ints(16), buf(2, 8), dma((3,))],
-            input_output_aliases={7: 0},
-            compiler_params=params(20),
-            cost_estimate=cost(100 if side == 0 else 1),
-        )(splat, *edge, got, bulk, ends, halo, out)
-    return out
+    bulk = [c1, c2]
+    return pl.pallas_call(
+        functools.partial(edge_kernel, spacing),
+        name="edge",
+        out_shape=f(2, n),
+        in_specs=[VMEM] * (9 + len(bulk)) + [ANY],
+        out_specs=ANY,
+        scratch_shapes=[buf(2, 2, 16), buf(2, 2, 2, 16), ints(2, 16), ints(2, 16), buf(4, 8), dma((4 + len(bulk),))],
+        input_output_aliases={9 + len(bulk): 0},
+        compiler_params=params(10),
+        cost_estimate=cost(1),
+    )(splat, buf0, regs0, buf1, regs1, got, ends, pack, dn, *bulk, out)
 
 
 def solution(mesh):

time: 28.3 us -> 28 us (0.989)
  the two profiles are of different devices: /device:TPU:6 before, /device:TPU:128 now
where the time goes in v3:
time: 28 us; the launch traced here: 27.8 us
  Pallas kernels  12.7 us (45%)
  starting transfers between devices  10.7 us (38%)
  waiting for transfers between devices  4.4 us (16%)
    pallas_call x2, Pallas kernels, chunk(): pl.pallas_call(functools.partial(chunk_kernel, base, part, lo, hi, spacin...  6.41 us
    ppermute x1, starting transfers between devices, body(): dn = lax.ppermute(dn, 'space', down)  5.02 us
    pallas_call x1, Pallas kernels, body(): pl.pallas_call(second_kernel, name='second', out_shape=[f(2, n), f(2, 8)]...  3.22 us
    ppermute x1, waiting for transfers between devices, body(): dn = lax.ppermute(dn, 'space', down)  3.18 us
    ppermute x1, starting transfers between devices, body(): pack = lax.ppermute(pack, 'space', up)  2.73 us
    pallas_call x1, Pallas kernels, body(): pl.pallas_call(functools.partial(edge_kernel, spacing), name='edge', out_...  1.64 us
    pallas_call x1, Pallas kernels, body(): pl.pallas_call(functools.partial(own_kernel, rows), name='own', out_shape...  1.43 us
    ppermute x1, waiting for transfers between devices, body(): pack = lax.ppermute(pack, 'space', up)  1.21 us
  transfers between devices with their start and end apart: 5, of which 2 were waited for; matrix products, arithmetic and copies ran while one was open for 0% of the time, Pallas kernels for 35%

profile of v3, /device:TPU:128, one launch (start us, length us, event | category | flops | bytes accessed | tf_op | source)
XLA Modules:
  0.0 27.8 jit_solution(16239763971514609413)
XLA Ops:
  0.0 1.4 %own.1 = (f32[6,8,1024]{2,1,0:T(8,128)S(1)}, s32[136,1024]{1,0:T(8,128)S(1)}, s32[136,1024]{1,0:T(8,128)S(1)}, f32[16,8,128]{2,1,0:T(8,128)S(1)}) custom-call(f32[8]{0:T(128)} %rho_tab.1, f32[8]{0:T(128)} %cond_tab.1, f32[2,256,1024]{2,1,0:T(8,128)} %end.5, f32[2,2,256,1024]{3,2,1,0:T(8,128)} %source.5, s32[256,1024]{1,0:T(8,128)} %region.5, s32[256,1024]{1,0:T(8,128)} %diri.5), custom_call_target="tpu_custom_call" | custom-call | flops 4000 | bytes 3000 | tf_op jit(solution)/shard_map/own/pallas_call | solution.py:407
  1.4 1.0 %collective-permute-start = (f32[6,8,1024]{2,1,0:T(8,128)S(1)}, f32[6,8,1024]{2,1,0:T(8,128)S(1)}, u32[]{:S(2)}, u32[]{:S(2)}) collective-permute-start(f32[6,8,1024]{2,1,0:T(8,128)S(1)} %get-tuple-element.28.got), channel_id=1, source_target_pairs={{64,0},{128,64},{192,128},{0,192},{65,1},{129,65},{193,129},{1,193... | collective-permute-start | bytes 589832 | tf_op jit(solution)/shard_map/ppermute | solution.py:417
  2.4 3.3 %chunk.2 = (f32[7,136,1024]{2,1,0:T(8,128)S(1)}, f32[128,1024]{1,0:T(8,128)S(1)}, f32[3,8,1024]{2,1,0:T(8,128)S(1)}, s32[2,8,1024]{2,1,0:T(8,128)S(1)}, s32[136,...) custom-call(f32[16,8,128]{2,1,0:T(8,128)S(1)} %get-tuple-element.25.splat, s32[136,1024]{1,0:T(8,128)S(1)} %get-tuple-element.26.reg_v, ...), custom_call_target="tpu_custom_call" | custom-call | flops 4000 | bytes 3000 | tf_op jit(solution)/shard_map/chunk/pallas_call | solution.py:420
  5.7 0.8 %collective-permute-start.3 = (f32[128,1024]{1,0:T(8,128)S(1)}, f32[128,1024]{1,0:T(8,128)S(1)}, u32[]{:S(2)}, u32[]{:S(2)}) collective-permute-start(f32[128,1024]{1,0:T(8,128)S(1)} %get-tuple-element.42), channel_id=1, source_target_pairs={{64,0},{128,64},{192,128},{0,192},{65,1},{129,65},{193,129},{1,193... | collective-permute-start | bytes 1572872 | tf_op jit(solution)/shard_map/ppermute | solution.py:445
  6.5 0.0 collective-permute-done.got
  6.5 3.2 %chunk.3 = (f32[7,136,1024]{2,1,0:T(8,128)S(1)}, f32[128,1024]{1,0:T(8,128)S(1)}, f32[3,8,1024]{2,1,0:T(8,128)S(1)}, s32[2,8,1024]{2,1,0:T(8,128)S(1)}, f32[24,1...) custom-call(f32[16,8,128]{2,1,0:T(8,128)S(1)} %get-tuple-element.25.splat, ...), custom_call_target="tpu_custom_call" | custom-call | flops 4000 | bytes 3000 | tf_op jit(solution)/shard_map/chunk/pallas_call | solution.py:420
  9.7 1.2 %collective-permute-start.4 = (f32[128,1024]{1,0:T(8,128)S(1)}, f32[128,1024]{1,0:T(8,128)S(1)}, u32[]{:S(2)}, u32[]{:S(2)}) collective-permute-start(f32[128,1024]{1,0:T(8,128)S(1)} %get-tuple-element.43), channel_id=1, source_target_pairs={{64,0},{128,64},{192,128},{0,192},{65,1},{129,65},{193,129},{1,193... | collective-permute-start | bytes 1572872 | tf_op jit(solution)/shard_map/ppermute | solution.py:446
  10.8 2.7 %collective-permute-start.1 = (f32[24,1024]{1,0:T(8,128)S(1)}, f32[24,1024]{1,0:T(8,128)S(1)}, u32[]{:S(2)}, u32[]{:S(2)}) collective-permute-start(f32[24,1024]{1,0:T(8,128)S(1)} %pack.1.refs_0_), channel_id=1, source_target_pairs={{0,1},{1,2},{2,3},{3,4},{4,5},{5,6},{6,7},{7,8},{8,9},{9,10},{10,1... | collective-permute-start | bytes 294920 | tf_op jit(solution)/shard_map/ppermute | solution.py:447
  13.5 5.0 %collective-permute-start.2 = (f32[24,1024]{1,0:T(8,128)S(1)}, f32[24,1024]{1,0:T(8,128)S(1)}, u32[]{:S(2)}, u32[]{:S(2)}) collective-permute-start(f32[24,1024]{1,0:T(8,128)S(1)} %get-tuple-element.41), channel_id=1, source_target_pairs={{1,0},{2,1},{3,2},{4,3},{5,4},{6,5},{7,6},{8,7},{9,8},{10,9},{11,1... | collective-permute-start | bytes 294920 | tf_op jit(solution)/shard_map/ppermute | solution.py:448
  18.6 3.2 %second.1 = (f32[2,256,1024]{2,1,0:T(8,128)}, f32[2,8,1024]{2,1,0:T(8,128)S(1)}) custom-call(f32[7,136,1024]{2,1,0:T(8,128)S(1)} %get-tuple-element.35.w1, f32[7,136,1024]{2,1,0:T(8,128)S(1)} %get-tuple-element.36.w2, f32[8,272,128]{2,1,0:T(8,128)S(1)} %get-tuple-element.37.x1, f32[256,1024]{1,0:T(8,128)S(1)} %get-tuple-element.38.s0, ...), custom_call_target="tpu_custom_call" | custom-call | flops 4000 | bytes 3000 | tf_op jit(solution)/shard_map/second/pallas_call | solution.py:450
  21.8 1.2 %collective-permute-done.1.from_up = f32[24,1024]{1,0:T(8,128)S(1)} collective-permute-done((f32[24,1024]{1,0:T(8,128)S(1)}, f32[24,1024]{1,0:T(8,128)S(1)}, u32[]{:S(2)}, u32[]{:S(2)}) %collective-permute-start.1) | collective-permute-done | bytes 98336 | tf_op jit(solution)/shard_map/ppermute | solution.py:447
  23.0 3.2 %collective-permute-done.2.from_down = f32[24,1024]{1,0:T(8,128)S(1)} collective-permute-done((f32[24,1024]{1,0:T(8,128)S(1)}, f32[24,1024]{1,0:T(8,128)S(1)}, u32[]{:S(2)}, u32[]{:S(2)}) %collective-permute-start.2) | collective-permute-done | bytes 98336 | tf_op jit(solution)/shard_map/ppermute | solution.py:448
  26.2 0.0 collective-permute-done.3.refs_0_
  26.2 0.0 collective-permute-done.4.refs_1_
  26.2 1.6 %edge.1 = f32[2,256,1024]{2,1,0:T(8,128)} custom-call(f32[16,8,128]{2,1,0:T(8,128)S(1)} %get-tuple-element.25.splat, f32[3,8,1024]{2,1,0:T(8,128)S(1)} %get-tuple-element.33.own0, s32[2,8,1024]{2,1,0:T(8,128)S(1)} %get-tuple-element.34.regs0, f32[3,8,1024]{2,1,0:T(8,128)S(1)} %get-tuple-element.31.buf.own1, ...), custom_call_target="tpu_custom_call", output_to_operand_aliasing={{}: (11, {})} | custom-call | flops 4000 | bytes 3000 | tf_op jit(solution)/shard_map/edge/pallas_call | solution.py:462
  (1 shorter events, 0.0 us)
Async XLA Ops:
  1.4 5.0 %collective-permute-start = (f32[6,8,1024]{2,1,0:T(8,128)S(1)}, f32[6,8,1024]{2,1,0:T(8,128)S(1)}, u32[]{:S(2)}, u32[]{:S(2)}) collective-permute-start(f32[6,8,1024]{2,1,0:T(8,128)S(1)} %get-tuple-element.28.got), channel_id=1, source_target_pairs={{64,0},{128,64},{192,128},{0,192},{65,1},{129,65},{193,129},{1,193... | collective-permute-start | bytes 589832 | tf_op jit(solution)/shard_map/ppermute | solution.py:417
  5.7 20.5 %collective-permute-start.3 = (f32[128,1024]{1,0:T(8,128)S(1)}, f32[128,1024]{1,0:T(8,128)S(1)}, u32[]{:S(2)}, u32[]{:S(2)}) collective-permute-start(f32[128,1024]{1,0:T(8,128)S(1)} %get-tuple-element.42), channel_id=1, source_target_pairs={{64,0},{128,64},{192,128},{0,192},{65,1},{129,65},{193,129},{1,193... | collective-permute-start | bytes 1572872 | tf_op jit(solution)/shard_map/ppermute | solution.py:445
  9.7 16.5 %collective-permute-start.4 = (f32[128,1024]{1,0:T(8,128)S(1)}, f32[128,1024]{1,0:T(8,128)S(1)}, u32[]{:S(2)}, u32[]{:S(2)}) collective-permute-start(f32[128,1024]{1,0:T(8,128)S(1)} %get-tuple-element.43), channel_id=1, source_target_pairs={{64,0},{128,64},{192,128},{0,192},{65,1},{129,65},{193,129},{1,193... | collective-permute-start | bytes 1572872 | tf_op jit(solution)/shard_map/ppermute | solution.py:446
  10.8 12.2 %collective-permute-start.1 = (f32[24,1024]{1,0:T(8,128)S(1)}, f32[24,1024]{1,0:T(8,128)S(1)}, u32[]{:S(2)}, u32[]{:S(2)}) collective-permute-start(f32[24,1024]{1,0:T(8,128)S(1)} %pack.1.refs_0_), channel_id=1, source_target_pairs={{0,1},{1,2},{2,3},{3,4},{4,5},{5,6},{6,7},{7,8},{8,9},{9,10},{10,1... | collective-permute-start | bytes 294920 | tf_op jit(solution)/shard_map/ppermute | solution.py:447
  13.5 12.6 %collective-permute-start.2 = (f32[24,1024]{1,0:T(8,128)S(1)}, f32[24,1024]{1,0:T(8,128)S(1)}, u32[]{:S(2)}, u32[]{:S(2)}) collective-permute-start(f32[24,1024]{1,0:T(8,128)S(1)} %get-tuple-element.41), channel_id=1, source_target_pairs={{1,0},{2,1},{3,2},{4,3},{5,4},{6,5},{7,6},{8,7},{9,8},{10,9},{11,1... | collective-permute-start | bytes 294920 | tf_op jit(solution)/shard_map/ppermute | solution.py:448
